TPU v7x, 256 devices: a whole 4x4x8 slice. The times are simulated.
256 devices in a mesh: ta: 8 (over z_lo, core), ha: 8 (over z_hi, y), wa: 4 (over x).
Axes of the slice: x: 4, y: 4, z: 8 (z_hi: 2, z_lo: 4; z = z_hi * 4 + z_lo), core: 2. Of those that a mesh axis runs over, the one named last changes fastest.
Arguments:
- query: bfloat16 [16, 32, 64, 1536], P('ta', 'ha', 'wa')
- key: bfloat16 [16, 32, 64, 1536], P('ta', 'ha', 'wa')
- value: bfloat16 [16, 32, 64, 1536], P('ta', 'ha', 'wa'), may hold values from -6 to 6
- d_out: bfloat16 [16, 32, 64, 1536], P('ta', 'ha', 'wa'), may hold values from -6 to 6
- text_key: bfloat16 [256, 1536], P(('ta', 'ha', 'wa')), may hold values from -6 to 6
- text_value: bfloat16 [256, 1536], P(('ta', 'ha', 'wa')), may hold values from -6 to 6
- block_pattern: int32 [8, 16, 16, 27], P('ta', 'ha', 'wa'), may hold values from 0 to 1, as said below
- text_length: int32 [1], replicated, may hold values from 32 to 256
Outputs:
- attended: bfloat16 [16, 32, 64, 1536], P('ta', 'ha', 'wa')
- query_grad: bfloat16 [16, 32, 64, 1536], P('ta', 'ha', 'wa')
- key_grad: bfloat16 [16, 32, 64, 1536], P('ta', 'ha', 'wa')
- value_grad: bfloat16 [16, 32, 64, 1536], P('ta', 'ha', 'wa')
- text_key_grad: bfloat16 [256, 1536], P(('ta', 'ha', 'wa'))
- text_value_grad: bfloat16 [256, 1536], P(('ta', 'ha', 'wa'))
Inputs may be any that keep to these rules, and one draw needn't show every extreme that they name: `block_pattern`: entry 13 (offset 0, 0, 0) is always 1.
All inputs are finite; a program needn't handle non-finite values.
Results may differ from a plain program's by a relative error of at most 0.013.
Values may be sent and summed in bfloat16 or wider, within the bound.
No kernel may reach another device: no remote copies, remote signals or barrier semaphores. Data moves between devices by JAX's collectives and lax.ppermute only.
A program may use at most 192 MiB of HBM per device.

v0:
```python
import functools

import jax
import jax.numpy as jnp
import numpy as np
from jax import lax
from jax.experimental import pallas as pl
from jax.experimental.pallas import tpu as pltpu
from jax.sharding import PartitionSpec as P

HEAD = 128
PAIR = 2 * HEAD
TILE_T = 2
TILE_H = 2
TILE_W = 4
TILE = TILE_T * TILE_H * TILE_W
NEGATIVE = -1e30
LOG2E = 1.4426950408889634
EXTRA = 16
PACKS = 2
VMEM = 58 * 1024 * 1024
F32 = jnp.float32
BF16 = jnp.bfloat16

ROWS = 4
COLS = 16
TILES_H = ROWS // TILE_H
TILES_W = COLS // TILE_W
CUBE = TILE_T * ROWS * COLS
GROUP = 4
GROUP_H = GROUP * TILES_H
OWN = GROUP_H * TILES_W * TILE
SIDE = GROUP_H * TILE
RIM = (TILES_W + 2) * TILE
ALL = OWN + 2 * SIDE + RIM
SEEN = (TILES_H + 2) * (TILES_W + 2)


def natural_index(row):
    tile_h = row >> 6
    tile_w = (row >> 4) & 3
    t = (row >> 3) & 1
    h = (row >> 2) & 1
    w = row & 3
    return t * (ROWS * COLS) + (tile_h * TILE_H + h) * COLS + tile_w * TILE_W + w


def pack_kernel(first_ref, second_ref, *rest):
    out_ref = rest[-1]
    row = lax.broadcasted_iota(jnp.int32, (CUBE, CUBE), 0)
    col = lax.broadcasted_iota(jnp.int32, (CUBE, CUBE), 1)
    order = jnp.where(natural_index(row) == col, 1.0, 0.0).astype(BF16)
    first = jnp.dot(order, first_ref[...], preferred_element_type=F32).astype(BF16)
    second = jnp.dot(order, second_ref[...], preferred_element_type=F32).astype(BF16)
    groups, _, width = out_ref.shape
    heads = width // PAIR
    for group in range(groups):
        for i in range(heads):
            source = slice((group * heads + i) * HEAD, (group * heads + i + 1) * HEAD)
            out_ref[group, :CUBE, i * PAIR : i * PAIR + HEAD] = first[:, source]
            out_ref[group, :CUBE, i * PAIR + HEAD : (i + 1) * PAIR] = second[:, source]
        if len(rest) > 1:
            pattern = rest[0][...].astype(F32)
            lines = jnp.concatenate([pattern, jnp.zeros_like(pattern)], 0).astype(BF16)
            out_ref[group, CUBE:, :] = jnp.zeros((EXTRA, width), BF16)
            out_ref[group, CUBE:, : pattern.shape[1]] = lines


def pack(first, second, pattern=None):
    width = first.shape[1] // GROUP
    step = GROUP // PACKS
    rows = CUBE + (0 if pattern is None else EXTRA)
    specs = [pl.BlockSpec((CUBE, width * step), lambda g: (0, g))] * 2
    extras = ()
    if pattern is not None:
        specs.append(pl.BlockSpec(pattern.shape, lambda g: (0, 0)))
        extras = (pattern,)
    return pl.pallas_call(
        pack_kernel,
        grid=(PACKS,),
        in_specs=specs,
        out_specs=pl.BlockSpec((step, rows, 2 * width), lambda g: (g, 0, 0)),
        out_shape=jax.ShapeDtypeStruct((GROUP, rows, 2 * width), BF16),
        compiler_params=pltpu.CompilerParams(vmem_limit_bytes=VMEM),
    )(first, second, *extras)


def unpack_kernel(packed_ref, first_ref, second_ref):
    row = lax.broadcasted_iota(jnp.int32, (CUBE, CUBE), 0)
    col = lax.broadcasted_iota(jnp.int32, (CUBE, CUBE), 1)
    order = jnp.where(natural_index(col) == row, 1.0, 0.0).astype(BF16)
    groups, _, width = packed_ref.shape
    heads = width // PAIR
    for group in range(groups):
        both = jnp.dot(order, packed_ref[group], preferred_element_type=F32).astype(BF16)
        for i in range(heads):
            target = slice((group * heads + i) * HEAD, (group * heads + i + 1) * HEAD)
            first_ref[:, target] = both[:, i * PAIR : i * PAIR + HEAD]
            second_ref[:, target] = both[:, i * PAIR + HEAD : (i + 1) * PAIR]


def unpack(packed):
    _, rows, width = packed.shape
    step = GROUP // PACKS
    half = width // 2
    return pl.pallas_call(
        unpack_kernel,
        grid=(PACKS,),
        in_specs=[pl.BlockSpec((step, rows, width), lambda g: (g, 0, 0))],
        out_specs=[pl.BlockSpec((CUBE, half * step), lambda g: (0, g))] * 2,
        out_shape=[jax.ShapeDtypeStruct((CUBE, GROUP * half), BF16)] * 2,
        compiler_params=pltpu.CompilerParams(vmem_limit_bytes=VMEM),
    )(packed)


def block_rows(block):
    low, high = block * TILES_H - 1, (block + 1) * TILES_H + 1
    outer = -1 if low < 0 else GROUP_H if high > GROUP_H else None
    return max(low, 0), min(high, GROUP_H), outer


def seen_tiles(block):
    low, high, outer = block_rows(block)
    tiles = [(h, w) for h in range(low, high) for w in range(TILES_W)]
    tiles += [(h, -1) for h in range(low, high)] + [(h, TILES_W) for h in range(low, high)]
    if outer is not None:
        tiles += [(outer, w) for w in (*range(TILES_W), -1, TILES_W)]
    return tiles


def attention_kernel(
    text_bits,
    length_ref,
    allow_ref,
    qg_ref,
    here_ref,
    below_ref,
    above_ref,
    text_ref,
    od_ref,
    here_out,
    below_out,
    above_out,
    text_out,
    text_away_out,
    below_sum,
    above_sum,
):
    text_count = text_ref.shape[0]
    scale = HEAD**-0.5
    near = (here_ref, below_ref, above_ref)
    sums = (here_out, below_sum, above_sum)
    text_row = lax.broadcasted_iota(jnp.int32, (text_count, CUBE), 0)
    text_place = jnp.zeros_like(text_row)
    for bit, place in enumerate(text_bits):
        text_place += ((text_row >> bit) & 1) << place
    text_ok = (text_place ^ length_ref[1]) < length_ref[0]
    blank = jnp.zeros((CUBE, HEAD), BF16)
    text_kv = text_ref[...]
    line = TILES_W * TILE
    def look(block):
        low, high, outer = block_rows(block)
        count = high - low
        q = qg_ref[block, :, :HEAD]
        g = qg_ref[block, :, HEAD:]
        both = jnp.concatenate(
            [jnp.concatenate([q, blank], 1), jnp.concatenate([blank, g], 1)], 0
        )
        done = 0 if block == 0 else 2
        places = [(low * line, count * line, done * line)]
        for side in range(2):
            places.append((OWN + side * (SIDE + TILE) + low * TILE, count * TILE, done * TILE))
        if outer is not None:
            rim = (OWN + 2 * (SIDE + TILE), OWN + SIDE, OWN + 2 * SIDE + TILE)
            for first, size in zip(rim, (line, TILE, TILE)):
                places.append((first, size, 0 if block == 0 else size))
        keys = []
        masks = []
        for i in range(3):
            parts = [near[i][first : first + size, :] for first, size, _ in places]
            keys.append(jnp.concatenate(parts, 0))
            tiles = allow_ref[block, i * SEEN : (i + 1) * SEEN, :]
            spread = jnp.broadcast_to(tiles[:, None, :], (SEEN, TILE, CUBE))
            masks.append(spread.reshape(SEEN * TILE, CUBE) > 0.5)
        keys.append(text_kv)
        masks.append(text_ok)
        scores = []
        dprobs = []
        for kv, ok in zip(keys, masks):
            mixed = lax.dot_general(
                kv, both, (((1,), (1,)), ((), ())), preferred_element_type=F32
            )
            scores.append(jnp.where(ok, mixed[:, :HEAD] * (scale * LOG2E), NEGATIVE))
            dprobs.append(mixed[:, HEAD:])
        top = functools.reduce(jnp.maximum, [jnp.max(s, 0, keepdims=True) for s in scores])
        return g, both, places, keys, scores, dprobs, top

    def finish(block, found):
        g, both, places, keys, scores, dprobs, top = found
        exps = [jnp.exp2(s - top) for s in scores]
        total = functools.reduce(jnp.add, [jnp.sum(e, 0, keepdims=True) for e in exps])
        inverse = 1.0 / total
        weights = [(e * inverse).astype(BF16) for e in exps]
        attended = jnp.zeros((CUBE, HEAD), F32)
        for w, kv in zip(weights, keys):
            attended += lax.dot_general(
                w, kv[:, HEAD:], (((0,), (0,)), ((), ())), preferred_element_type=F32
            )
        attended = attended.astype(BF16)
        od_ref[block, :, :HEAD] = attended
        product = g.astype(F32) * attended.astype(F32)
        delta = jnp.sum(product.T, 0, keepdims=True)
        dscores = [(e * ((d - delta) * inverse)).astype(BF16) for e, d in zip(exps, dprobs)]
        return both, places, keys, weights, dscores

    def settle_block(block, state):
        both, places, keys, weights, dscores = state
        query_grad = jnp.zeros((CUBE, HEAD), F32)
        for d, kv in zip(dscores, keys):
            query_grad += lax.dot_general(
                d, kv[:, :HEAD], (((0,), (0,)), ((), ())), preferred_element_type=F32
            )
        od_ref[block, :, HEAD:] = (query_grad * scale).astype(BF16)
        for i in range(4):
            change = jnp.dot(
                jnp.concatenate([dscores[i], weights[i]], 1), both, preferred_element_type=F32
            )
            if i == 3:
                middle = text_count // 2
                for target, piece in (
                    (text_out, change[:middle]),
                    (text_away_out, change[middle:]),
                ):
                    if block == 0:
                        target[...] = piece
                    else:
                        target[...] += piece
                continue
            taken = 0
            target = sums[i]
            for first, size, old in places:
                if old:
                    target[first : first + old, :] += change[taken : taken + old]
                if old < size:
                    target[first + old : first + size, :] = change[taken + old : taken + size]
                taken += size
    found = look(0)
    before = None
    for block in range(GROUP):
        following = look(block + 1) if block + 1 < GROUP else None
        now = finish(block, found)
        if before is not None:
            settle_block(block - 1, before)
        before = now
        found = following
    settle_block(GROUP - 1, before)
    lane = lax.broadcasted_iota(jnp.int32, (1, PAIR), 1)
    factor = jnp.where(lane < HEAD, scale, 1.0).astype(F32)
    here_out[...] = here_out[...] * factor
    below_out[...] = (below_sum[...] * factor).astype(BF16)
    above_out[...] = (above_sum[...] * factor).astype(BF16)
    text_out[...] = text_out[...] * factor
    text_away_out[...] = text_away_out[...] * factor


def attention(length, allow, qg, here, below, above, text, text_bits):
    width = qg.shape[-1]
    heads = width // PAIR
    text_count = text.shape[0]

    def spec(rows):
        return pl.BlockSpec((rows, PAIR), lambda h: (0, h))

    def shape(rows, dtype):
        return jax.ShapeDtypeStruct((rows, width), dtype)

    part = pl.BlockSpec((GROUP, CUBE, PAIR), lambda h: (0, 0, h))
    return pl.pallas_call(
        functools.partial(attention_kernel, text_bits),
        grid=(heads,),
        in_specs=[
            pl.BlockSpec(memory_space=pltpu.SMEM),
            pl.BlockSpec(allow.shape, lambda h: (0, 0, 0)),
            part,
        ]
        + [spec(ALL)] * 3
        + [spec(text_count)],
        out_specs=[part] + [spec(ALL)] * 3 + [spec(text_count // 2)] * 2,
        out_shape=[
            jax.ShapeDtypeStruct(qg.shape, BF16),
            shape(ALL, F32),
            shape(ALL, BF16),
            shape(ALL, BF16),
            shape(text_count // 2, F32),
            shape(text_count // 2, F32),
        ],
        scratch_shapes=[pltpu.VMEM((rows, PAIR), F32) for rows in (ALL, ALL)],
        compiler_params=pltpu.CompilerParams(vmem_limit_bytes=VMEM),
    )(length, allow, qg, here, below, above, text)


def settle_kernel(half_ref, own_ref, first_ref, second_ref, rim_ref, left_ref, right_ref, out_ref):
    line = TILES_W * TILE
    rim = rim_ref[...].astype(F32)
    half = half_ref[0]
    groups = out_ref.shape[0]
    for group in range(groups):
        block = pl.program_id(0) * groups + group
        cube = slice(group * CUBE, (group + 1) * CUBE)
        total = own_ref[cube] + first_ref[cube].astype(F32) + second_ref[cube].astype(F32)
        for i in range(TILES_H):
            edge = (block == 0) & (half == 1) if i == 0 else (block == GROUP - 1) & (half == 0)
            part = total[i * line : (i + 1) * line]
            part += jnp.where(edge, rim, 0.0)
            here = slice((group * TILES_H + i) * TILE, (group * TILES_H + i + 1) * TILE)
            pieces = [
                part[:TILE] + left_ref[here].astype(F32),
                part[TILE : line - TILE],
                part[line - TILE :] + right_ref[here].astype(F32),
            ]
            out_ref[group, i * line : (i + 1) * line, :] = jnp.concatenate(pieces, 0).astype(BF16)


def settle(half, own, first, second, rim, left, right):
    width = own.shape[-1]
    step = GROUP // PACKS

    def spec(rows):
        return pl.BlockSpec((rows * step, width), lambda b: (b, 0))

    return pl.pallas_call(
        settle_kernel,
        grid=(PACKS,),
        in_specs=[
            pl.BlockSpec(memory_space=pltpu.SMEM),
            spec(CUBE),
            spec(CUBE),
            spec(CUBE),
            pl.BlockSpec((TILES_W * TILE, width), lambda b: (0, 0)),
            spec(TILES_H * TILE),
            spec(TILES_H * TILE),
        ],
        out_specs=pl.BlockSpec((step, CUBE, width), lambda b: (b, 0, 0)),
        out_shape=jax.ShapeDtypeStruct((GROUP, CUBE, width), BF16),
        compiler_params=pltpu.CompilerParams(vmem_limit_bytes=VMEM),
    )(half, own, first, second, rim, left, right)


def offset_table():
    table = np.full((GROUP, 3, SEEN, TILES_H, TILES_W), -1, np.int32)
    for block in range(GROUP):
        for k, (kh, kw) in enumerate(seen_tiles(block)):
            for qh in range(TILES_H):
                for qw in range(TILES_W):
                    dh, dw = kh - (block * TILES_H + qh), kw - qw
                    if abs(dh) <= 1 and abs(dw) <= 1:
                        for i, dt in enumerate((0, -1, 1)):
                            table[block, i, k, qh, qw] = 9 * dt + 3 * dh + dw + 13
    return table


def allowed_tiles(pattern, half):
    hot = offset_table().reshape(GROUP, 3, SEEN, -1)[..., None] == np.arange(27)
    picked = jnp.sum(jnp.where(hot, pattern[:, None, None], 0.0), -1)
    places = np.array([seen_tiles(block) for block in range(GROUP)])
    t = lax.axis_index("ta") + jnp.array([0, -1, 1])
    t_ok = (t >= 0) & (t < lax.axis_size("ta"))
    w = lax.axis_index("wa") * TILES_W + places[..., 1]
    w_ok = (w >= 0) & (w < TILES_W * lax.axis_size("wa"))
    h = half * GROUP_H + places[..., 0]
    h_ok = (h >= 0) & (h < TILES_H * lax.axis_size("ha"))
    inside = t_ok[None, :, None] & (w_ok & h_ok)[:, None, :]
    picked = jnp.where(inside[..., None], picked, 0.0)
    return jnp.repeat(picked.reshape(GROUP, 3 * SEEN, -1), TILE, axis=2)


def turned_width(value, step):
    count = lax.axis_size("wa")
    return lax.ppermute(value, "wa", [(i, (i + step) % count) for i in range(count)])


def turned_time(value, step):
    count_t, count_h = lax.axis_size("ta"), lax.axis_size("ha")
    pairs = []
    for t in range(count_t):
        for h in range(count_h):
            t_to = t + step
            h_to = h
            if not 0 <= t_to < count_t:
                h_to = (h + count_h // 2) % count_h
            pairs.append((t * count_h + h, t_to % count_t * count_h + h_to))
    return lax.ppermute(value, ("ta", "ha"), pairs)


def swapped(value, axis, bit):
    count = lax.axis_size(axis)
    return lax.ppermute(value, axis, [(i, i ^ bit) for i in range(count)])


def regrouped(value):
    count = lax.axis_size("ha")
    groups = [list(range(i, i + GROUP)) for i in range(0, count, GROUP)]
    return lax.all_to_all(value, "ha", 0, 0, axis_index_groups=groups)


def log2(count):
    return count.bit_length() - 1


def text_steps():
    ta, ha, wa = (lax.axis_size(axis) for axis in ("ta", "ha", "wa"))
    halves = [("ha", ha >> i) for i in range(1, log2(ha) + 1)]
    steps = halves[:-2] + [("ta", ta >> i) for i in range(1, log2(ta))] + halves[-2:]
    steps += [("wa", wa >> i) for i in range(1, log2(wa) + 1)]
    return steps + [("ta", 1)]


def text_bits():
    start = {"wa": 0, "ha": log2(lax.axis_size("wa"))}
    start["ta"] = start["ha"] + log2(lax.axis_size("ha"))
    return tuple(start[axis] + log2(bit) for axis, bit in text_steps())


def is_high(axis, bit):
    return (lax.axis_index(axis) & bit) > 0


def gather_text(value, axis, bit):
    high = is_high(axis, bit)
    mine = theirs = value
    if axis == "ha" and bit < GROUP:
        middle = value.shape[0] // 2
        mine = jnp.where(high, value[middle:], value[:middle])
        theirs = jnp.where(high, value[:middle], value[middle:])
    return jnp.concatenate([mine, swapped(theirs, axis, bit)], 1)


def scatter_text(mine, theirs, axis, bit):
    high = is_high(axis, bit)
    other = swapped(theirs, axis, bit)
    if axis == "ha" and bit < GROUP:
        first = jnp.where(high, other, mine)
        second = jnp.where(high, mine, other)
        return jnp.concatenate([first, second], 0)
    return mine + other


def scatter_halves(value, axis, bit):
    middle = value.shape[1] // 2
    return scatter_text(value[:, :middle], value[:, middle:], axis, bit)


def after(value, *others):
    return lax.optimization_barrier((value, *others))[0]


def local(query, key, value, d_out, text_key, text_value, block_pattern, text_length):
    full = query.shape[-1]
    half = lax.axis_index("ha") // GROUP
    steps = text_steps()
    line = TILES_W * TILE

    kv_out = pack(
        key.reshape(CUBE, full), value.reshape(CUBE, full), block_pattern.reshape(-1, 27)
    )
    text = jnp.stack([text_key.reshape(-1, HEAD), text_value.reshape(-1, HEAD)], 1)
    text = after(text.reshape(GROUP, 1, -1), kv_out)
    for step in steps[:2]:
        text = gather_text(text, *step)
    qg_out = pack(query.reshape(CUBE, full), d_out.reshape(CUBE, full))
    kv_in = regrouped(kv_out)
    width = kv_in.shape[-1]

    own = kv_in[:, :CUBE].reshape(GROUP_H, TILES_W, TILE, width)
    flat = own.reshape(OWN, width)
    edge = jnp.where(half == 0, own[GROUP_H - 1], own[0])
    rim = swapped(edge.reshape(line, width), "ha", GROUP)
    text = gather_text(after(text, kv_in, qg_out), *steps[2])
    to_right = jnp.concatenate([own[:, TILES_W - 1].reshape(SIDE, width), rim[line - TILE :]], 0)
    to_left = jnp.concatenate([own[:, 0].reshape(SIDE, width), rim[:TILE]], 0)
    left = turned_width(to_right, 1)
    right = turned_width(to_left, -1)
    text = after(text, rim)
    for step in steps[3:5]:
        text = gather_text(text, *step)
    here = after(jnp.concatenate([flat, left, right, rim], 0), text)
    below = turned_time(here, 1)
    above = turned_time(here, -1)
    qg = regrouped(after(qg_out, rim))
    text = after(text, here)
    text = gather_text(text, *steps[5])
    text = after(text, qg)
    for step in steps[6:]:
        text = gather_text(text, *step)
    allow = allowed_tiles(kv_in[:, CUBE : CUBE + 8, :27].astype(F32), half)

    me = (lax.axis_index("ta") * lax.axis_size("ha") + lax.axis_index("ha")) * lax.axis_size("wa")
    me = me + lax.axis_index("wa")
    od, here_grad, below_grad, above_grad, text_grad, text_away = attention(
        jnp.concatenate([text_length, me.reshape(1)]),
        allow,
        qg,
        here,
        below,
        above,
        text[0],
        text_bits(),
    )

    first = turned_time(below_grad, -1)
    second = turned_time(above_grad, 1)
    back = steps[::-1]
    text_grad = scatter_text(text_grad[None], text_away[None], *back[0])
    text_grad = scatter_halves(text_grad, *back[1])
    od_in = regrouped(od)
    text_grad = scatter_halves(after(text_grad, od_in), *back[2])
    halo = here_grad[OWN:] + first[OWN:].astype(F32) + second[OWN:].astype(F32)
    side = SIDE + TILE
    to_left = halo[:side].astype(BF16)
    to_right = halo[side : 2 * side].astype(BF16)
    rim_grad = halo[2 * side :]
    right = turned_width(to_left, -1)
    left = turned_width(to_right, 1)
    text_grad = scatter_halves(after(text_grad, to_left, to_right), *back[3])
    rim_out = jnp.concatenate(
        [
            rim_grad[:TILE] + left[SIDE:].astype(F32),
            rim_grad[TILE : line - TILE],
            rim_grad[line - TILE :] + right[SIDE:].astype(F32),
        ],
        0,
    ).astype(BF16)
    rim_in = swapped(rim_out, "ha", GROUP)
    text_grad = scatter_halves(after(text_grad, rim_out), *back[4])
    text_grad = scatter_halves(after(text_grad, rim_in), *back[5])
    grads = settle(half.reshape(1), here_grad, first, second, rim_in, left, right)
    text_grad = after(text_grad, grads)
    for step in back[6:]:
        text_grad = scatter_halves(text_grad, *step)
    attended, query_grad = unpack(od_in)
    key_grad, value_grad = unpack(regrouped(grads))
    text_grad = text_grad.astype(BF16).reshape(-1, 2, HEAD)
    return (
        attended.reshape(query.shape),
        query_grad.reshape(query.shape),
        key_grad.reshape(query.shape),
        value_grad.reshape(query.shape),
        text_grad[:, 0].reshape(1, full),
        text_grad[:, 1].reshape(1, full),
    )


def solution(mesh):
    cube = P("ta", "ha", "wa", None)
    text = P(("ta", "ha", "wa"), None)
    return jax.shard_map(
        local,
        mesh=mesh,
        in_specs=(cube, cube, cube, cube, text, text, cube, P()),
        out_specs=(cube, cube, cube, cube, text, text),
        check_vma=False,
    )
```

profile of v0, /device:TPU:32, one launch (start us, length us, event | category | flops | bytes accessed | tf_op | source)
XLA Modules:
  0.0 155.5 jit_solution(12520267011619423598)
XLA Ops:
  0.7 2.3 %shard_map.163 = bf16[4,144,768]{2,1,0:T(8,128)(2,1)} custom-call(bf16[128,1536]{1,0:T(8,128)(2,1)} %bitcast.36, bf16[128,1536]{1,0:T(8,128)(2,1)} %bitcast.37, s32[8,27]{1,0:T(8,128)} %bitcast.43), custom_call_target="tpu_custom_call" | custom-call | tf_op jit(solution)/shard_map/pallas_call | solution.py:78
  3.0 4.5 %all-to-all-start = ((bf16[4,144,768]{2,1,0:T(8,128)(2,1)}), bf16[4,144,768]{2,1,0:T(8,128)(2,1)S(1)}, u32[]{:S(2)}, u32[]{:S(2)}) async-start(bf16[4,144,768]{2,1,0:T(8,128)(2,1)} %shard_map.163), calls=%async_computation | async-start | bytes 1769472 | tf_op jit(solution)/shard_map/all_to_all | solution.py:403
  7.5 6.4 %collective-permute-start.3 = (bf16[4,1,768]{2,1,0:T(2,128)(2,1)S(1)}, bf16[4,1,768]{2,1,0:T(2,128)(2,1)S(1)}, u32[]{:S(2)}, u32[]{:S(2)}) collective-permute-start(bf16[4,1,768]{2,1,0:T(2,128)(2,1)S(1)} %copy.37), channel_id=1, source_target_pairs={{0,16},{4,20},{8,24},{12,28},{16,0},{20,4},{24,8},{28,12},{1,17},{... | collective-permute-start | bytes 18440 | tf_op jit(solution)/shard_map/ppermute | solution.py:397
  15.6 3.0 %collective-permute-start.4 = (bf16[4,2,768]{2,1,0:T(2,128)(2,1)S(1)}, bf16[4,2,768]{2,1,0:T(2,128)(2,1)S(1)}, u32[]{:S(2)}, u32[]{:S(2)}) collective-permute-start(bf16[4,2,768]{2,1,0:T(2,128)(2,1)S(1)} %pad_maximum_fusion.12), channel_id=1, source_target_pairs={{0,128},{32,160},{64,192},{96,224},{128,0},{160,32},{192,64},{224,... | collective-permute-start | bytes 36872 | tf_op jit(solution)/shard_map/ppermute | solution.py:397
  18.6 2.3 %shard_map.164 = bf16[4,128,768]{2,1,0:T(8,128)(2,1)} custom-call(bf16[128,1536]{1,0:T(8,128)(2,1)} %bitcast.38, bf16[128,1536]{1,0:T(8,128)(2,1)} %bitcast.39), custom_call_target="tpu_custom_call" | custom-call | tf_op jit(solution)/shard_map/pallas_call | solution.py:78
  21.6 6.7 %collective-permute-start = (bf16[64,768]{1,0:T(8,128)(2,1)S(1)}, bf16[64,768]{1,0:T(8,128)(2,1)S(1)}, u32[]{:S(2)}, u32[]{:S(2)}) collective-permute-start(bf16[64,768]{1,0:T(8,128)(2,1)S(1)} %bitcast.40), channel_id=1, source_target_pairs={{0,16},{4,20},{8,24},{12,28},{16,0},{20,4},{24,8},{28,12},{1,17},{... | collective-permute-start | bytes 294920 | tf_op jit(solution)/shard_map/ppermute | solution.py:397
  28.4 2.9 %collective-permute-done = bf16[64,768]{1,0:T(8,128)(2,1)S(1)} collective-permute-done((bf16[64,768]{1,0:T(8,128)(2,1)S(1)}, bf16[64,768]{1,0:T(8,128)(2,1)S(1)}, u32[]{:S(2)}, u32[]{:S(2)}) %collective-permute-start) | collective-permute-done | bytes 98336 | tf_op jit(solution)/shard_map/ppermute | solution.py:397
  31.3 2.6 %collective-permute-start.6 = (bf16[2,8,768]{2,1,0:T(8,128)(2,1)S(1)}, bf16[2,8,768]{2,1,0:T(8,128)(2,1)S(1)}, u32[]{:S(2)}, u32[]{:S(2)}) collective-permute-start(bf16[2,8,768]{2,1,0:T(8,128)(2,1)S(1)} %get-tuple-element.67), channel_id=1, source_target_pairs={{0,8},{4,12},{8,0},{12,4},{16,24},{20,28},{24,16},{28,20},{1,9},{5... | collective-permute-start | bytes 73736 | tf_op jit(solution)/shard_map/ppermute | solution.py:397
  33.9 2.8 %collective-permute-start.2 = (bf16[144,768]{1,0:T(8,128)(2,1)S(1)}, bf16[144,768]{1,0:T(8,128)(2,1)S(1)}, u32[]{:S(2)}, u32[]{:S(2)}) collective-permute-start(bf16[144,768]{1,0:T(8,128)(2,1)S(1)} %pad_maximum_fusion.2), channel_id=1, source_target_pairs={{0,3},{1,0},{2,1},{3,2},{4,7},{5,4},{6,5},{7,6},{8,11},{9,8},{10,9... | collective-permute-start | bytes 663560 | tf_op jit(solution)/shard_map/ppermute | solution.py:379
  37.8 3.0 %collective-permute-done.7 = bf16[1,16,768]{2,1,0:T(8,128)(2,1)S(1)} collective-permute-done((bf16[1,16,768]{2,1,0:T(8,128)(2,1)S(1)}, bf16[1,16,768]{2,1,0:T(8,128)(2,1)S(1)}, u32[]{:S(2)}, u32[]{:S(2)}) %collective-permute-start.7) | collective-permute-done | bytes 24608 | tf_op jit(solution)/shard_map/ppermute | solution.py:397
  41.4 2.5 %collective-permute-done.1 = bf16[144,768]{1,0:T(8,128)(2,1)S(1)} collective-permute-done((bf16[144,768]{1,0:T(8,128)(2,1)S(1)}, bf16[144,768]{1,0:T(8,128)(2,1)S(1)}, u32[]{:S(2)}, u32[]{:S(2)}) %collective-permute-start.1) | collective-permute-done | bytes 221216 | tf_op jit(solution)/shard_map/ppermute | solution.py:379
  45.3 3.5 %all-to-all-start.1 = ((bf16[4,128,768]{2,1,0:T(8,128)(2,1)}), bf16[4,128,768]{2,1,0:T(8,128)(2,1)S(1)}, u32[]{:S(2)}, u32[]{:S(2)}) async-start(bf16[4,128,768]{2,1,0:T(8,128)(2,1)} %shard_map.164), calls=%async_computation.1 | async-start | bytes 1572864 | tf_op jit(solution)/shard_map/all_to_all | solution.py:403
  50.3 5.0 %collective-permute-done.10 = bf16[1,32,768]{2,1,0:T(8,128)(2,1)S(1)} collective-permute-done((bf16[1,32,768]{2,1,0:T(8,128)(2,1)S(1)}, bf16[1,32,768]{2,1,0:T(8,128)(2,1)S(1)}, u32[]{:S(2)}, u32[]{:S(2)}) %collective-permute-start.10) | collective-permute-done | bytes 49184 | tf_op jit(solution)/shard_map/ppermute | solution.py:397
  55.4 5.9 %all-to-all-done.1.qg_ref = bf16[4,128,768]{2,1,0:T(8,128)(2,1)S(1)} async-done(((bf16[4,128,768]{2,1,0:T(8,128)(2,1)}), bf16[4,128,768]{2,1,0:T(8,128)(2,1)S(1)}, u32[]{:S(2)}, u32[]{:S(2)}) %all-to-all-start.1) | async-done | bytes 786464 | tf_op jit(solution)/shard_map/all_to_all | solution.py:403
  61.7 5.1 %collective-permute-done.11 = bf16[1,64,768]{2,1,0:T(8,128)(2,1)S(1)} collective-permute-done((bf16[1,64,768]{2,1,0:T(8,128)(2,1)S(1)}, bf16[1,64,768]{2,1,0:T(8,128)(2,1)S(1)}, u32[]{:S(2)}, u32[]{:S(2)}) %collective-permute-start.11) | collective-permute-done | bytes 98336 | tf_op jit(solution)/shard_map/ppermute | solution.py:397
  69.2 13.9 %shard_map.165 = (bf16[4,128,768]{2,1,0:T(8,128)(2,1)}, f32[864,768]{1,0:T(8,128)}, bf16[864,768]{1,0:T(8,128)(2,1)}, bf16[864,768]{1,0:T(8,128)(2,1)}, f32[128,768]{1,0:T(8,128)}, /*index=5*/f32[128,768]{1,0:T(8,128)}) custom-call(s32[2]{0:T(128)} %pad_add_fusion.length_ref, f32[4,72,128]{2,1,0:T(8,128)} %copy.38.allow_ref, bf16[4,128,768]{2,1,0:T(8,128)(2,1)} %copy-done.3, ...), custom_call_target="tpu_custom_call" | custom-call | tf_op jit(solution)/shard_map/pallas_call | solution.py:278
  85.3 3.5 %all-to-all-start.2 = ((bf16[4,128,768]{2,1,0:T(8,128)(2,1)}), bf16[4,128,768]{2,1,0:T(8,128)(2,1)S(1)}, u32[]{:S(2)}, u32[]{:S(2)}) async-start(bf16[4,128,768]{2,1,0:T(8,128)(2,1)} %get-tuple-element.35), calls=%async_computation.2 | async-start | bytes 1572864 | tf_op jit(solution)/shard_map/all_to_all | solution.py:403
  90.2 7.5 %collective-permute-done.19 = f32[1,64,768]{2,1,0:T(8,128)S(1)} collective-permute-done((f32[1,64,768]{2,1,0:T(8,128)S(1)}, f32[1,64,768]{2,1,0:T(8,128)S(1)}, u32[]{:S(2)}, u32[]{:S(2)}) %collective-permute-start.19) | collective-permute-done | bytes 196640 | tf_op jit(solution)/shard_map/ppermute | solution.py:397
  98.4 3.9 %all-to-all-done.2.packed_ref = bf16[4,128,768]{2,1,0:T(8,128)(2,1)S(1)} async-done(((bf16[4,128,768]{2,1,0:T(8,128)(2,1)}), bf16[4,128,768]{2,1,0:T(8,128)(2,1)S(1)}, u32[]{:S(2)}, u32[]{:S(2)}) %all-to-all-start.2) | async-done | bytes 786464 | tf_op jit(solution)/shard_map/all_to_all | solution.py:403
  103.6 5.8 %collective-permute-done.20 = f32[1,32,768]{2,1,0:T(8,128)S(1)} collective-permute-done((f32[1,32,768]{2,1,0:T(8,128)S(1)}, f32[1,32,768]{2,1,0:T(8,128)S(1)}, u32[]{:S(2)}, u32[]{:S(2)}) %collective-permute-start.20) | collective-permute-done | bytes 98336 | tf_op jit(solution)/shard_map/ppermute | solution.py:397
  110.3 2.2 %fusion.8 = (bf16[352,768]{1,0:T(8,128)(2,1)S(1)}, f32[352,768]{1,0:T(8,128)S(1)}) fusion(bf16[864,768]{1,0:T(8,128)(2,1)S(1)} %collective-permute-done.14.second_ref, bf16[864,768]{1,0:T(8,128)(2,1)S(1)} %collective-permute-done.13.first_ref, f32[864,768]{1,0:T(8,128)} %get-tuple-element.38.own_ref), kind=kLoop, calls=%fused_computation.55 | loop fusion | flops 1351680 | bytes 3784704 | tf_op jit(solution)/shard_map/convert.5
  113.6 2.9 %collective-permute-start.16 = (bf16[144,768]{1,0:T(8,128)(2,1)S(1)}, bf16[144,768]{1,0:T(8,128)(2,1)S(1)}, u32[]{:S(2)}, u32[]{:S(2)}) collective-permute-start(bf16[144,768]{1,0:T(8,128)(2,1)S(1)} %get-tuple-element.57), channel_id=1, source_target_pairs={{0,3},{1,0},{2,1},{3,2},{4,7},{5,4},{6,5},{7,6},{8,11},{9,8},{10,9... | collective-permute-start | bytes 663560 | tf_op jit(solution)/shard_map/ppermute | solution.py:379
  116.8 3.6 %collective-permute-done.15.left_ref = bf16[144,768]{1,0:T(8,128)(2,1)S(1)} collective-permute-done((bf16[144,768]{1,0:T(8,128)(2,1)S(1)}, bf16[144,768]{1,0:T(8,128)(2,1)S(1)}, u32[]{:S(2)}, u32[]{:S(2)}) %collective-permute-start.15) | collective-permute-done | bytes 221216 | tf_op jit(solution)/shard_map/ppermute | solution.py:379
  120.5 2.1 %collective-permute-start.22 = (f32[2,8,768]{2,1,0:T(8,128)S(1)}, f32[2,8,768]{2,1,0:T(8,128)S(1)}, u32[]{:S(2)}, u32[]{:S(2)}) collective-permute-start(f32[2,8,768]{2,1,0:T(8,128)S(1)} %slice.153), channel_id=1, source_target_pairs={{0,8},{4,12},{8,0},{12,4},{16,24},{20,28},{24,16},{28,20},{1,9},{5... | collective-permute-start | bytes 147464 | tf_op jit(solution)/shard_map/ppermute | solution.py:397
  122.6 5.8 %collective-permute-start.17 = (bf16[64,768]{1,0:T(8,128)(2,1)S(1)}, bf16[64,768]{1,0:T(8,128)(2,1)S(1)}, u32[]{:S(2)}, u32[]{:S(2)}) collective-permute-start(bf16[64,768]{1,0:T(8,128)(2,1)S(1)} %pad_maximum_fusion.5), channel_id=1, source_target_pairs={{0,16},{4,20},{8,24},{12,28},{16,0},{20,4},{24,8},{28,12},{1,17},{... | collective-permute-start | bytes 294920 | tf_op jit(solution)/shard_map/ppermute | solution.py:397
  128.4 3.8 %collective-permute-done.17.rim_ref = bf16[64,768]{1,0:T(8,128)(2,1)S(1)} collective-permute-done((bf16[64,768]{1,0:T(8,128)(2,1)S(1)}, bf16[64,768]{1,0:T(8,128)(2,1)S(1)}, u32[]{:S(2)}, u32[]{:S(2)}) %collective-permute-start.17) | collective-permute-done | bytes 98336 | tf_op jit(solution)/shard_map/ppermute | solution.py:397
  133.9 2.9 %shard_map.167 = bf16[4,128,768]{2,1,0:T(8,128)(2,1)} custom-call(s32[1]{0:T(128)} %bitcast.18.half_ref, f32[864,768]{1,0:T(8,128)} %get-tuple-element.38.own_ref, bf16[864,768]{1,0:T(8,128)(2,1)} %copy-done.4, bf16[864,768]{1,0:T(8,128)(2,1)} %copy-done.5, bf16[64,768]{1,0:T(8,128)(2,1)} %copy-done.10, bf16[144,768]{1,0:T(8,128)(2,1)} %copy-done.7, ...), custom_call_target="tpu_custom_call" | custom-call | tf_op jit(solution)/shard_map/pallas_call | solution.py:331
  138.3 3.5 %all-to-all-start.3 = ((bf16[4,128,768]{2,1,0:T(8,128)(2,1)}), bf16[4,128,768]{2,1,0:T(8,128)(2,1)S(1)}, u32[]{:S(2)}, u32[]{:S(2)}) async-start(bf16[4,128,768]{2,1,0:T(8,128)(2,1)} %shard_map.167), calls=%async_computation.3 | async-start | bytes 1572864 | tf_op jit(solution)/shard_map/all_to_all | solution.py:403
  141.9 5.6 %collective-permute-start.25 = (f32[4,1,768]{2,1,0:T(1,128)S(1)}, f32[4,1,768]{2,1,0:T(1,128)S(1)}, u32[]{:S(2)}, u32[]{:S(2)}) collective-permute-start(f32[4,1,768]{2,1,0:T(1,128)S(1)} %slice.185), channel_id=1, source_target_pairs={{0,16},{4,20},{8,24},{12,28},{16,0},{20,4},{24,8},{28,12},{1,17},{... | collective-permute-start | bytes 36872 | tf_op jit(solution)/shard_map/ppermute | solution.py:397
  147.4 2.3 %shard_map.166 = (bf16[128,1536]{1,0:T(8,128)(2,1)}, bf16[128,1536]{1,0:T(8,128)(2,1)}) custom-call(bf16[4,128,768]{2,1,0:T(8,128)(2,1)} %copy-done.1), custom_call_target="tpu_custom_call" | custom-call | tf_op jit(solution)/shard_map/pallas_call | solution.py:106
  150.4 2.0 %all-to-all-done.3.packed_ref = bf16[4,128,768]{2,1,0:T(8,128)(2,1)S(1)} async-done(((bf16[4,128,768]{2,1,0:T(8,128)(2,1)}), bf16[4,128,768]{2,1,0:T(8,128)(2,1)S(1)}, u32[]{:S(2)}, u32[]{:S(2)}) %all-to-all-start.3) | async-done | bytes 786464 | tf_op jit(solution)/shard_map/all_to_all | solution.py:403
  153.3 2.3 %shard_map.168 = (bf16[128,1536]{1,0:T(8,128)(2,1)}, bf16[128,1536]{1,0:T(8,128)(2,1)}) custom-call(bf16[4,128,768]{2,1,0:T(8,128)(2,1)} %copy-done.2), custom_call_target="tpu_custom_call" | custom-call | tf_op jit(solution)/shard_map/pallas_call | solution.py:106
  (123 shorter events, 21.7 us)
Async XLA Ops:
  3.0 18.0 %all-to-all-start = ((bf16[4,144,768]{2,1,0:T(8,128)(2,1)}), bf16[4,144,768]{2,1,0:T(8,128)(2,1)S(1)}, u32[]{:S(2)}, u32[]{:S(2)}) async-start(bf16[4,144,768]{2,1,0:T(8,128)(2,1)} %shard_map.163), calls=%async_computation | async-start | bytes 1769472 | tf_op jit(solution)/shard_map/all_to_all | solution.py:403
  7.5 8.1 %collective-permute-start.3 = (bf16[4,1,768]{2,1,0:T(2,128)(2,1)S(1)}, bf16[4,1,768]{2,1,0:T(2,128)(2,1)S(1)}, u32[]{:S(2)}, u32[]{:S(2)}) collective-permute-start(bf16[4,1,768]{2,1,0:T(2,128)(2,1)S(1)} %copy.37), channel_id=1, source_target_pairs={{0,16},{4,20},{8,24},{12,28},{16,0},{20,4},{24,8},{28,12},{1,17},{... | collective-permute-start | bytes 18440 | tf_op jit(solution)/shard_map/ppermute | solution.py:397
  15.6 5.3 %collective-permute-start.4 = (bf16[4,2,768]{2,1,0:T(2,128)(2,1)S(1)}, bf16[4,2,768]{2,1,0:T(2,128)(2,1)S(1)}, u32[]{:S(2)}, u32[]{:S(2)}) collective-permute-start(bf16[4,2,768]{2,1,0:T(2,128)(2,1)S(1)} %pad_maximum_fusion.12), channel_id=1, source_target_pairs={{0,128},{32,160},{64,192},{96,224},{128,0},{160,32},{192,64},{224,... | collective-permute-start | bytes 36872 | tf_op jit(solution)/shard_map/ppermute | solution.py:397
  21.0 7.4 %collective-permute-start.5 = (bf16[4,4,768]{2,1,0:T(4,128)(2,1)S(1)}, bf16[4,4,768]{2,1,0:T(4,128)(2,1)S(1)}, u32[]{:S(2)}, u32[]{:S(2)}) collective-permute-start(bf16[4,4,768]{2,1,0:T(4,128)(2,1)S(1)} %pad_maximum_fusion.11), channel_id=1, source_target_pairs={{0,64},{32,96},{64,0},{96,32},{128,192},{160,224},{192,128},{224,1... | collective-permute-start | bytes 73736 | tf_op jit(solution)/shard_map/ppermute | solution.py:397
  21.6 9.7 %collective-permute-start = (bf16[64,768]{1,0:T(8,128)(2,1)S(1)}, bf16[64,768]{1,0:T(8,128)(2,1)S(1)}, u32[]{:S(2)}, u32[]{:S(2)}) collective-permute-start(bf16[64,768]{1,0:T(8,128)(2,1)S(1)} %bitcast.40), channel_id=1, source_target_pairs={{0,16},{4,20},{8,24},{12,28},{16,0},{20,4},{24,8},{28,12},{1,17},{... | collective-permute-start | bytes 294920 | tf_op jit(solution)/shard_map/ppermute | solution.py:397
  31.3 5.6 %collective-permute-start.6 = (bf16[2,8,768]{2,1,0:T(8,128)(2,1)S(1)}, bf16[2,8,768]{2,1,0:T(8,128)(2,1)S(1)}, u32[]{:S(2)}, u32[]{:S(2)}) collective-permute-start(bf16[2,8,768]{2,1,0:T(8,128)(2,1)S(1)} %get-tuple-element.67), channel_id=1, source_target_pairs={{0,8},{4,12},{8,0},{12,4},{16,24},{20,28},{24,16},{28,20},{1,9},{5... | collective-permute-start | bytes 73736 | tf_op jit(solution)/shard_map/ppermute | solution.py:397
  33.9 7.5 %collective-permute-start.2 = (bf16[144,768]{1,0:T(8,128)(2,1)S(1)}, bf16[144,768]{1,0:T(8,128)(2,1)S(1)}, u32[]{:S(2)}, u32[]{:S(2)}) collective-permute-start(bf16[144,768]{1,0:T(8,128)(2,1)S(1)} %pad_maximum_fusion.2), channel_id=1, source_target_pairs={{0,3},{1,0},{2,1},{3,2},{4,7},{5,4},{6,5},{7,6},{8,11},{9,8},{10,9... | collective-permute-start | bytes 663560 | tf_op jit(solution)/shard_map/ppermute | solution.py:379
  36.7 7.2 %collective-permute-start.1 = (bf16[144,768]{1,0:T(8,128)(2,1)S(1)}, bf16[144,768]{1,0:T(8,128)(2,1)S(1)}, u32[]{:S(2)}, u32[]{:S(2)}) collective-permute-start(bf16[144,768]{1,0:T(8,128)(2,1)S(1)} %pad_maximum_fusion.1), channel_id=1, source_target_pairs={{0,1},{1,2},{2,3},{3,0},{4,5},{5,6},{6,7},{7,4},{8,9},{9,10},{10,1... | collective-permute-start | bytes 663560 | tf_op jit(solution)/shard_map/ppermute | solution.py:379
  36.9 3.9 %collective-permute-start.7 = (bf16[1,16,768]{2,1,0:T(8,128)(2,1)S(1)}, bf16[1,16,768]{2,1,0:T(8,128)(2,1)S(1)}, u32[]{:S(2)}, u32[]{:S(2)}) collective-permute-start(bf16[1,16,768]{2,1,0:T(8,128)(2,1)S(1)} %get-tuple-element.65), channel_id=1, source_target_pairs={{0,4},{4,0},{8,12},{12,8},{16,20},{20,16},{24,28},{28,24},{1,5},{5... | collective-permute-start | bytes 73736 | tf_op jit(solution)/shard_map/ppermute | solution.py:397
  44.1 22.8 %copy-start = (bf16[864,768]{1,0:T(8,128)(2,1)}, bf16[864,768]{1,0:T(8,128)(2,1)S(1)}, u32[]{:S(2)}) copy-start(bf16[864,768]{1,0:T(8,128)(2,1)S(1)} %pad_maximum_fusion.here_ref) | copy-start | bytes 3981316
  44.1 17.2 %copy-start.6 = (pred[4,3,24,8,27]{4,3,2,1,0:T(8,128)(4,1)S(1)}, pred[4,3,24,8,27]{4,3,2,1,0:T(8,128)(4,1)}, u32[]{:S(2)}) copy-start(pred[4,3,24,8,27]{4,3,2,1,0:T(8,128)(4,1)} %constant.50.clone) | copy-start | bytes 186628
  44.1 25.1 %collective-permute-start.9 = (bf16[864,768]{1,0:T(8,128)(2,1)S(1)}, bf16[864,768]{1,0:T(8,128)(2,1)}, u32[]{:S(2)}, u32[]{:S(2)}) collective-permute-start(bf16[864,768]{1,0:T(8,128)(2,1)S(1)} %pad_maximum_fusion.here_ref), channel_id=1, source_target_pairs={{0,240},{4,244},{8,248},{12,252},{16,224},{20,228},{24,232},{28,23... | collective-permute-start | bytes 3981320 | tf_op jit(solution)/shard_map/ppermute | solution.py:392
  44.1 25.1 %collective-permute-start.8 = (bf16[864,768]{1,0:T(8,128)(2,1)S(1)}, bf16[864,768]{1,0:T(8,128)(2,1)}, u32[]{:S(2)}, u32[]{:S(2)}) collective-permute-start(bf16[864,768]{1,0:T(8,128)(2,1)S(1)} %pad_maximum_fusion.here_ref), channel_id=1, source_target_pairs={{0,32},{4,36},{8,40},{12,44},{16,48},{20,52},{24,56},{28,60},{32,6... | collective-permute-start | bytes 3981320 | tf_op jit(solution)/shard_map/ppermute | solution.py:392
  45.3 16.0 %all-to-all-start.1 = ((bf16[4,128,768]{2,1,0:T(8,128)(2,1)}), bf16[4,128,768]{2,1,0:T(8,128)(2,1)S(1)}, u32[]{:S(2)}, u32[]{:S(2)}) async-start(bf16[4,128,768]{2,1,0:T(8,128)(2,1)} %shard_map.164), calls=%async_computation.1 | async-start | bytes 1572864 | tf_op jit(solution)/shard_map/all_to_all | solution.py:403
  49.7 5.7 %collective-permute-start.10 = (bf16[1,32,768]{2,1,0:T(8,128)(2,1)S(1)}, bf16[1,32,768]{2,1,0:T(8,128)(2,1)S(1)}, u32[]{:S(2)}, u32[]{:S(2)}) collective-permute-start(bf16[1,32,768]{2,1,0:T(8,128)(2,1)S(1)} %copy-done.9), channel_id=1, source_target_pairs={{0,2},{1,3},{2,0},{3,1},{4,6},{5,7},{6,4},{7,5},{8,10},{9,11},{10,... | collective-permute-start | bytes 147464 | tf_op jit(solution)/shard_map/ppermute | solution.py:397
  61.3 5.6 %collective-permute-start.11 = (bf16[1,64,768]{2,1,0:T(8,128)(2,1)S(1)}, bf16[1,64,768]{2,1,0:T(8,128)(2,1)S(1)}, u32[]{:S(2)}, u32[]{:S(2)}) collective-permute-start(bf16[1,64,768]{2,1,0:T(8,128)(2,1)S(1)} %pad_maximum_fusion.4), channel_id=1, source_target_pairs={{0,1},{1,0},{2,3},{3,2},{4,5},{5,4},{6,7},{7,6},{8,9},{9,8},{10,11... | collective-permute-start | bytes 294920 | tf_op jit(solution)/shard_map/ppermute | solution.py:397
  66.9 1.5 collective-permute-start.12
  83.1 5.7 %collective-permute-start.18 = (f32[1,128,768]{2,1,0:T(8,128)}, f32[1,128,768]{2,1,0:T(8,128)}, u32[]{:S(2)}, u32[]{:S(2)}) collective-permute-start(f32[1,128,768]{2,1,0:T(8,128)} %bitcast.46), channel_id=1, source_target_pairs={{0,32},{32,0},{64,96},{96,64},{128,160},{160,128},{192,224},{224,1... | collective-permute-start | bytes 1179656 | tf_op jit(solution)/shard_map/ppermute | solution.py:397
  83.6 26.7 %collective-permute-start.13 = (bf16[864,768]{1,0:T(8,128)(2,1)}, bf16[864,768]{1,0:T(8,128)(2,1)S(1)}, u32[]{:S(2)}, u32[]{:S(2)}) collective-permute-start(bf16[864,768]{1,0:T(8,128)(2,1)} %get-tuple-element.39), channel_id=1, source_target_pairs={{0,240},{4,244},{8,248},{12,252},{16,224},{20,228},{24,232},{28,23... | collective-permute-start | bytes 3981320 | tf_op jit(solution)/shard_map/ppermute | solution.py:392
  85.3 25.0 %collective-permute-start.14 = (bf16[864,768]{1,0:T(8,128)(2,1)}, bf16[864,768]{1,0:T(8,128)(2,1)S(1)}, u32[]{:S(2)}, u32[]{:S(2)}) collective-permute-start(bf16[864,768]{1,0:T(8,128)(2,1)} %get-tuple-element.40), channel_id=1, source_target_pairs={{0,32},{4,36},{8,40},{12,44},{16,48},{20,52},{24,56},{28,60},{32,6... | collective-permute-start | bytes 3981320 | tf_op jit(solution)/shard_map/ppermute | solution.py:392
  85.3 16.9 %all-to-all-start.2 = ((bf16[4,128,768]{2,1,0:T(8,128)(2,1)}), bf16[4,128,768]{2,1,0:T(8,128)(2,1)S(1)}, u32[]{:S(2)}, u32[]{:S(2)}) async-start(bf16[4,128,768]{2,1,0:T(8,128)(2,1)} %get-tuple-element.35), calls=%async_computation.2 | async-start | bytes 1572864 | tf_op jit(solution)/shard_map/all_to_all | solution.py:403
  90.0 7.6 %collective-permute-start.19 = (f32[1,64,768]{2,1,0:T(8,128)S(1)}, f32[1,64,768]{2,1,0:T(8,128)S(1)}, u32[]{:S(2)}, u32[]{:S(2)}) collective-permute-start(f32[1,64,768]{2,1,0:T(8,128)S(1)} %slice.183), channel_id=1, source_target_pairs={{0,1},{1,0},{2,3},{3,2},{4,5},{5,4},{6,7},{7,6},{8,9},{9,8},{10,11... | collective-permute-start | bytes 589832 | tf_op jit(solution)/shard_map/ppermute | solution.py:397
  103.3 6.1 %collective-permute-start.20 = (f32[1,32,768]{2,1,0:T(8,128)S(1)}, f32[1,32,768]{2,1,0:T(8,128)S(1)}, u32[]{:S(2)}, u32[]{:S(2)}) collective-permute-start(f32[1,32,768]{2,1,0:T(8,128)S(1)} %slice.150), channel_id=1, source_target_pairs={{0,2},{1,3},{2,0},{3,1},{4,6},{5,7},{6,4},{7,5},{8,10},{9,11},{10,... | collective-permute-start | bytes 294920 | tf_op jit(solution)/shard_map/ppermute | solution.py:397
  112.6 4.2 %collective-permute-start.21 = (f32[1,16,768]{2,1,0:T(8,128)S(1)}, f32[1,16,768]{2,1,0:T(8,128)S(1)}, u32[]{:S(2)}, u32[]{:S(2)}) collective-permute-start(f32[1,16,768]{2,1,0:T(8,128)S(1)} %slice.151), channel_id=1, source_target_pairs={{0,4},{4,0},{8,12},{12,8},{16,20},{20,16},{24,28},{28,24},{1,5},{5... | collective-permute-start | bytes 147464 | tf_op jit(solution)/shard_map/ppermute | solution.py:397
  113.3 7.1 %collective-permute-start.15 = (bf16[144,768]{1,0:T(8,128)(2,1)S(1)}, bf16[144,768]{1,0:T(8,128)(2,1)S(1)}, u32[]{:S(2)}, u32[]{:S(2)}) collective-permute-start(bf16[144,768]{1,0:T(8,128)(2,1)S(1)} %get-tuple-element.56), channel_id=1, source_target_pairs={{0,1},{1,2},{2,3},{3,0},{4,5},{5,6},{6,7},{7,4},{8,9},{9,10},{10,1... | collective-permute-start | bytes 663560 | tf_op jit(solution)/shard_map/ppermute | solution.py:379
  113.6 6.8 %collective-permute-start.16 = (bf16[144,768]{1,0:T(8,128)(2,1)S(1)}, bf16[144,768]{1,0:T(8,128)(2,1)S(1)}, u32[]{:S(2)}, u32[]{:S(2)}) collective-permute-start(bf16[144,768]{1,0:T(8,128)(2,1)S(1)} %get-tuple-element.57), channel_id=1, source_target_pairs={{0,3},{1,0},{2,1},{3,2},{4,7},{5,4},{6,5},{7,6},{8,11},{9,8},{10,9... | collective-permute-start | bytes 663560 | tf_op jit(solution)/shard_map/ppermute | solution.py:379
  120.5 7.9 %collective-permute-start.22 = (f32[2,8,768]{2,1,0:T(8,128)S(1)}, f32[2,8,768]{2,1,0:T(8,128)S(1)}, u32[]{:S(2)}, u32[]{:S(2)}) collective-permute-start(f32[2,8,768]{2,1,0:T(8,128)S(1)} %slice.153), channel_id=1, source_target_pairs={{0,8},{4,12},{8,0},{12,4},{16,24},{20,28},{24,16},{28,20},{1,9},{5... | collective-permute-start | bytes 147464 | tf_op jit(solution)/shard_map/ppermute | solution.py:397
  122.6 9.6 %collective-permute-start.17 = (bf16[64,768]{1,0:T(8,128)(2,1)S(1)}, bf16[64,768]{1,0:T(8,128)(2,1)S(1)}, u32[]{:S(2)}, u32[]{:S(2)}) collective-permute-start(bf16[64,768]{1,0:T(8,128)(2,1)S(1)} %pad_maximum_fusion.5), channel_id=1, source_target_pairs={{0,16},{4,20},{8,24},{12,28},{16,0},{20,4},{24,8},{28,12},{1,17},{... | collective-permute-start | bytes 294920 | tf_op jit(solution)/shard_map/ppermute | solution.py:397
  132.3 4.5 %collective-permute-start.23 = (f32[4,4,768]{2,1,0:T(4,128)S(1)}, f32[4,4,768]{2,1,0:T(4,128)S(1)}, u32[]{:S(2)}, u32[]{:S(2)}) collective-permute-start(f32[4,4,768]{2,1,0:T(4,128)S(1)} %slice.156), channel_id=1, source_target_pairs={{0,64},{32,96},{64,0},{96,32},{128,192},{160,224},{192,128},{224,1... | collective-permute-start | bytes 147464 | tf_op jit(solution)/shard_map/ppermute | solution.py:397
  136.9 5.0 %collective-permute-start.24 = (f32[4,2,768]{2,1,0:T(2,128)S(1)}, f32[4,2,768]{2,1,0:T(2,128)S(1)}, u32[]{:S(2)}, u32[]{:S(2)}) collective-permute-start(f32[4,2,768]{2,1,0:T(2,128)S(1)} %slice.158), channel_id=1, source_target_pairs={{0,128},{32,160},{64,192},{96,224},{128,0},{160,32},{192,64},{224,... | collective-permute-start | bytes 73736 | tf_op jit(solution)/shard_map/ppermute | solution.py:397
  138.3 14.0 %all-to-all-start.3 = ((bf16[4,128,768]{2,1,0:T(8,128)(2,1)}), bf16[4,128,768]{2,1,0:T(8,128)(2,1)S(1)}, u32[]{:S(2)}, u32[]{:S(2)}) async-start(bf16[4,128,768]{2,1,0:T(8,128)(2,1)} %shard_map.167), calls=%async_computation.3 | async-start | bytes 1572864 | tf_op jit(solution)/shard_map/all_to_all | solution.py:403
  141.9 7.8 %collective-permute-start.25 = (f32[4,1,768]{2,1,0:T(1,128)S(1)}, f32[4,1,768]{2,1,0:T(1,128)S(1)}, u32[]{:S(2)}, u32[]{:S(2)}) collective-permute-start(f32[4,1,768]{2,1,0:T(1,128)S(1)} %slice.185), channel_id=1, source_target_pairs={{0,16},{4,20},{8,24},{12,28},{16,0},{20,4},{24,8},{28,12},{1,17},{... | collective-permute-start | bytes 36872 | tf_op jit(solution)/shard_map/ppermute | solution.py:397
  (14 other events, 104.6 us)
where the time goes:
time: 156 us
  starting transfers between devices  62.4 us (40%)
  waiting for transfers between devices  53.6 us (34%)
  Pallas kernels  26 us (17%)
  other arithmetic  7.82 us (5%)
  local copies, waits for them, and re-layouts  3.92 us (3%)
  between operations  1.72 us (1%)
    ppermute x18, starting transfers between devices, swapped(): return lax.ppermute(value, axis, [(i, i ^ bit) for i in range(count)])  39 us
    ppermute x18, waiting for transfers between devices, swapped(): return lax.ppermute(value, axis, [(i, i ^ bit) for i in range(count)])  35.7 us
    all_to_all x4, starting transfers between devices, regrouped(): return lax.all_to_all(value, 'ha', 0, 0, axis_index_groups=groups)  15 us
    pallas_call x1, Pallas kernels, attention(): pl.pallas_call(functools.partial(attention_kernel, text_bits), grid=(head...  13.9 us
    all_to_all x4, waiting for transfers between devices, regrouped(): return lax.all_to_all(value, 'ha', 0, 0, axis_index_groups=groups)  11.8 us
    ppermute x4, starting transfers between devices, turned_width(): lax.ppermute(value, 'wa', [(i, (i + step) % count) for i in range(count)])  6.15 us
    ppermute x4, waiting for transfers between devices, turned_width(): lax.ppermute(value, 'wa', [(i, (i + step) % count) for i in range(count)])  6.14 us
    pallas_call x2, Pallas kernels, pack(): pl.pallas_call(pack_kernel, grid=(PACKS,), in_specs=specs, out_specs=pl.B...  4.64 us
  transfers between devices with their start and end apart: 30, of which 15 were waited for; matrix products, arithmetic and copies ran while one was open for 5% of the time, Pallas kernels for 5%

commit v1 on v0

--- a/solution.py
+++ b/solution.py
@@ -435,19 +435,26 @@
     return jnp.concatenate([mine, swapped(theirs, axis, bit)], 1)
 
 
-def scatter_text(mine, theirs, axis, bit):
-    high = is_high(axis, bit)
-    other = swapped(theirs, axis, bit)
+def sent_text(mine, theirs, axis, bit):
+    return mine, swapped(theirs, axis, bit), axis, bit
+
+
+def joined_text(sent, *others):
+    mine, other, axis, bit = sent
+    if others:
+        mine, other = lax.optimization_barrier((mine, other, *others))[:2]
     if axis == "ha" and bit < GROUP:
+        high = is_high(axis, bit)
         first = jnp.where(high, other, mine)
         second = jnp.where(high, mine, other)
         return jnp.concatenate([first, second], 0)
     return mine + other
 
 
-def scatter_halves(value, axis, bit):
+def scatter_text(sent, axis, bit, *others):
+    value = joined_text(sent, *others)
     middle = value.shape[1] // 2
-    return scatter_text(value[:, :middle], value[:, middle:], axis, bit)
+    return sent_text(value[:, :middle], value[:, middle:], axis, bit)
 
 
 def after(value, *others):
@@ -488,10 +495,9 @@
     above = turned_time(here, -1)
     qg = regrouped(after(qg_out, rim))
     text = after(text, here)
-    text = gather_text(text, *steps[5])
-    text = after(text, qg)
-    for step in steps[6:]:
+    for step in steps[5:-1]:
         text = gather_text(text, *step)
+    text = gather_text(after(text, qg), *steps[-1])
     allow = allowed_tiles(kv_in[:, CUBE : CUBE + 8, :27].astype(F32), half)
 
     me = (lax.axis_index("ta") * lax.axis_size("ha") + lax.axis_index("ha")) * lax.axis_size("wa")
@@ -510,10 +516,10 @@
     first = turned_time(below_grad, -1)
     second = turned_time(above_grad, 1)
     back = steps[::-1]
-    text_grad = scatter_text(text_grad[None], text_away[None], *back[0])
-    text_grad = scatter_halves(text_grad, *back[1])
+    text_grad = sent_text(text_grad[None], text_away[None], *back[0])
+    text_grad = scatter_text(text_grad, *back[1])
     od_in = regrouped(od)
-    text_grad = scatter_halves(after(text_grad, od_in), *back[2])
+    text_grad = scatter_text(text_grad, *back[2], od_in)
     halo = here_grad[OWN:] + first[OWN:].astype(F32) + second[OWN:].astype(F32)
     side = SIDE + TILE
     to_left = halo[:side].astype(BF16)
@@ -521,7 +527,7 @@
     rim_grad = halo[2 * side :]
     right = turned_width(to_left, -1)
     left = turned_width(to_right, 1)
-    text_grad = scatter_halves(after(text_grad, to_left, to_right), *back[3])
+    text_grad = scatter_text(text_grad, *back[3], to_left, to_right)
     rim_out = jnp.concatenate(
         [
             rim_grad[:TILE] + left[SIDE:].astype(F32),
@@ -531,12 +537,11 @@
         0,
     ).astype(BF16)
     rim_in = swapped(rim_out, "ha", GROUP)
-    text_grad = scatter_halves(after(text_grad, rim_out), *back[4])
-    text_grad = scatter_halves(after(text_grad, rim_in), *back[5])
+    text_grad = scatter_text(text_grad, *back[4], rim_out)
+    text_grad = scatter_text(text_grad, *back[5], rim_in)
     grads = settle(half.reshape(1), here_grad, first, second, rim_in, left, right)
-    text_grad = after(text_grad, grads)
-    for step in back[6:]:
-        text_grad = scatter_halves(text_grad, *step)
+    text_grad = scatter_text(text_grad, *back[6], grads)
+    text_grad = joined_text(scatter_text(text_grad, *back[7]))
     attended, query_grad = unpack(od_in)
     key_grad, value_grad = unpack(regrouped(grads))
     text_grad = text_grad.astype(BF16).reshape(-1, 2, HEAD)

time: 156 us -> 147 us (0.942)
  waiting for transfers between devices: 53.6 us -> 47.3 us
  starting transfers between devices: 62.4 us -> 59.7 us
    ppermute x18, waiting for transfers between devices: 35.7 us -> 27.7 us  [swapped(): return lax.ppermute(value, axis, [(i, i ^ bit) for i in range(count)])]
    ppermute x18, starting transfers between devices: 39 us -> 36.1 us  [swapped(): return lax.ppermute(value, axis, [(i, i ^ bit) for i in range(count)])]
  transfers between devices with their start and end apart: 30 -> 30, of which waited for: 15 -> 14; matrix products, arithmetic and copies ran while one was open for 5% -> 6% of each run, Pallas kernels for 5% -> 5%
where the time goes in v1:
time: 147 us; the launch traced here: 146 us
  starting transfers between devices  59.7 us (41%)
  waiting for transfers between devices  47.3 us (32%)
  Pallas kernels  26 us (18%)
  other arithmetic  7.85 us (5%)
  local copies, waits for them, and re-layouts  3.71 us (3%)
  between operations  1.75 us (1%)
    ppermute x18, starting transfers between devices, swapped(): return lax.ppermute(value, axis, [(i, i ^ bit) for i in range(count)])  36.1 us
    ppermute x18, waiting for transfers between devices, swapped(): return lax.ppermute(value, axis, [(i, i ^ bit) for i in range(count)])  27.7 us
    all_to_all x4, starting transfers between devices, regrouped(): return lax.all_to_all(value, 'ha', 0, 0, axis_index_groups=groups)  14.9 us
    pallas_call x1, Pallas kernels, attention(): pl.pallas_call(functools.partial(attention_kernel, text_bits), grid=(head...  13.9 us
    all_to_all x4, waiting for transfers between devices, regrouped(): return lax.all_to_all(value, 'ha', 0, 0, axis_index_groups=groups)  12.8 us
    ppermute x4, waiting for transfers between devices, turned_width(): lax.ppermute(value, 'wa', [(i, (i + step) % count) for i in range(count)])  6.7 us
    ppermute x4, starting transfers between devices, turned_width(): lax.ppermute(value, 'wa', [(i, (i + step) % count) for i in range(count)])  6.23 us
    pallas_call x2, Pallas kernels, pack(): pl.pallas_call(pack_kernel, grid=(PACKS,), in_specs=specs, out_specs=pl.B...  4.62 us
  transfers between devices with their start and end apart: 30, of which 14 were waited for; matrix products, arithmetic and copies ran while one was open for 6% of the time, Pallas kernels for 5%

profile of v1, /device:TPU:32, one launch (start us, length us, event | category | flops | bytes accessed | tf_op | source)
XLA Modules:
  0.0 146.3 jit_solution(5821581494571020299)
XLA Ops:
  0.7 2.3 %shard_map.163 = bf16[4,144,768]{2,1,0:T(8,128)(2,1)} custom-call(bf16[128,1536]{1,0:T(8,128)(2,1)} %bitcast.36, bf16[128,1536]{1,0:T(8,128)(2,1)} %bitcast.37, s32[8,27]{1,0:T(8,128)} %bitcast.43), custom_call_target="tpu_custom_call" | custom-call | tf_op jit(solution)/shard_map/pallas_call | solution.py:78
  3.0 4.5 %all-to-all-start = ((bf16[4,144,768]{2,1,0:T(8,128)(2,1)}), bf16[4,144,768]{2,1,0:T(8,128)(2,1)S(1)}, u32[]{:S(2)}, u32[]{:S(2)}) async-start(bf16[4,144,768]{2,1,0:T(8,128)(2,1)} %shard_map.163), calls=%async_computation | async-start | bytes 1769472 | tf_op jit(solution)/shard_map/all_to_all | solution.py:403
  7.5 6.4 %collective-permute-start.3 = (bf16[4,1,768]{2,1,0:T(2,128)(2,1)S(1)}, bf16[4,1,768]{2,1,0:T(2,128)(2,1)S(1)}, u32[]{:S(2)}, u32[]{:S(2)}) collective-permute-start(bf16[4,1,768]{2,1,0:T(2,128)(2,1)S(1)} %copy.37), channel_id=1, source_target_pairs={{0,16},{4,20},{8,24},{12,28},{16,0},{20,4},{24,8},{28,12},{1,17},{... | collective-permute-start | bytes 18440 | tf_op jit(solution)/shard_map/ppermute | solution.py:397
  13.9 1.7 %collective-permute-done.3 = bf16[4,1,768]{2,1,0:T(2,128)(2,1)S(1)} collective-permute-done((bf16[4,1,768]{2,1,0:T(2,128)(2,1)S(1)}, bf16[4,1,768]{2,1,0:T(2,128)(2,1)S(1)}, u32[]{:S(2)}, u32[]{:S(2)}) %collective-permute-start.3) | collective-permute-done | bytes 6176 | tf_op jit(solution)/shard_map/ppermute | solution.py:397
  15.6 3.0 %collective-permute-start.4 = (bf16[4,2,768]{2,1,0:T(2,128)(2,1)S(1)}, bf16[4,2,768]{2,1,0:T(2,128)(2,1)S(1)}, u32[]{:S(2)}, u32[]{:S(2)}) collective-permute-start(bf16[4,2,768]{2,1,0:T(2,128)(2,1)S(1)} %pad_maximum_fusion.12), channel_id=1, source_target_pairs={{0,128},{32,160},{64,192},{96,224},{128,0},{160,32},{192,64},{224,... | collective-permute-start | bytes 36872 | tf_op jit(solution)/shard_map/ppermute | solution.py:397
  18.6 2.3 %shard_map.164 = bf16[4,128,768]{2,1,0:T(8,128)(2,1)} custom-call(bf16[128,1536]{1,0:T(8,128)(2,1)} %bitcast.38, bf16[128,1536]{1,0:T(8,128)(2,1)} %bitcast.39), custom_call_target="tpu_custom_call" | custom-call | tf_op jit(solution)/shard_map/pallas_call | solution.py:78
  21.6 6.7 %collective-permute-start = (bf16[64,768]{1,0:T(8,128)(2,1)S(1)}, bf16[64,768]{1,0:T(8,128)(2,1)S(1)}, u32[]{:S(2)}, u32[]{:S(2)}) collective-permute-start(bf16[64,768]{1,0:T(8,128)(2,1)S(1)} %bitcast.40), channel_id=1, source_target_pairs={{0,16},{4,20},{8,24},{12,28},{16,0},{20,4},{24,8},{28,12},{1,17},{... | collective-permute-start | bytes 294920 | tf_op jit(solution)/shard_map/ppermute | solution.py:397
  28.3 2.9 %collective-permute-done = bf16[64,768]{1,0:T(8,128)(2,1)S(1)} collective-permute-done((bf16[64,768]{1,0:T(8,128)(2,1)S(1)}, bf16[64,768]{1,0:T(8,128)(2,1)S(1)}, u32[]{:S(2)}, u32[]{:S(2)}) %collective-permute-start) | collective-permute-done | bytes 98336 | tf_op jit(solution)/shard_map/ppermute | solution.py:397
  31.3 2.6 %collective-permute-start.6 = (bf16[2,8,768]{2,1,0:T(8,128)(2,1)S(1)}, bf16[2,8,768]{2,1,0:T(8,128)(2,1)S(1)}, u32[]{:S(2)}, u32[]{:S(2)}) collective-permute-start(bf16[2,8,768]{2,1,0:T(8,128)(2,1)S(1)} %get-tuple-element.87), channel_id=1, source_target_pairs={{0,8},{4,12},{8,0},{12,4},{16,24},{20,28},{24,16},{28,20},{1,9},{5... | collective-permute-start | bytes 73736 | tf_op jit(solution)/shard_map/ppermute | solution.py:397
  33.9 2.8 %collective-permute-start.2 = (bf16[144,768]{1,0:T(8,128)(2,1)S(1)}, bf16[144,768]{1,0:T(8,128)(2,1)S(1)}, u32[]{:S(2)}, u32[]{:S(2)}) collective-permute-start(bf16[144,768]{1,0:T(8,128)(2,1)S(1)} %pad_maximum_fusion.2), channel_id=1, source_target_pairs={{0,3},{1,0},{2,1},{3,2},{4,7},{5,4},{6,5},{7,6},{8,11},{9,8},{10,9... | collective-permute-start | bytes 663560 | tf_op jit(solution)/shard_map/ppermute | solution.py:379
  37.8 3.0 %collective-permute-done.7 = bf16[1,16,768]{2,1,0:T(8,128)(2,1)S(1)} collective-permute-done((bf16[1,16,768]{2,1,0:T(8,128)(2,1)S(1)}, bf16[1,16,768]{2,1,0:T(8,128)(2,1)S(1)}, u32[]{:S(2)}, u32[]{:S(2)}) %collective-permute-start.7) | collective-permute-done | bytes 24608 | tf_op jit(solution)/shard_map/ppermute | solution.py:397
  40.8 3.2 %collective-permute-done.1 = bf16[144,768]{1,0:T(8,128)(2,1)S(1)} collective-permute-done((bf16[144,768]{1,0:T(8,128)(2,1)S(1)}, bf16[144,768]{1,0:T(8,128)(2,1)S(1)}, u32[]{:S(2)}, u32[]{:S(2)}) %collective-permute-start.1) | collective-permute-done | bytes 221216 | tf_op jit(solution)/shard_map/ppermute | solution.py:379
  47.0 3.5 %all-to-all-start.1 = ((bf16[4,128,768]{2,1,0:T(8,128)(2,1)}), bf16[4,128,768]{2,1,0:T(8,128)(2,1)S(1)}, u32[]{:S(2)}, u32[]{:S(2)}) async-start(bf16[4,128,768]{2,1,0:T(8,128)(2,1)} %shard_map.164), calls=%async_computation.1 | async-start | bytes 1572864 | tf_op jit(solution)/shard_map/all_to_all | solution.py:403
  50.6 5.6 %collective-permute-done.10 = bf16[1,32,768]{2,1,0:T(8,128)(2,1)S(1)} collective-permute-done((bf16[1,32,768]{2,1,0:T(8,128)(2,1)S(1)}, bf16[1,32,768]{2,1,0:T(8,128)(2,1)S(1)}, u32[]{:S(2)}, u32[]{:S(2)}) %collective-permute-start.10) | collective-permute-done | bytes 49184 | tf_op jit(solution)/shard_map/ppermute | solution.py:397
  56.8 5.1 %collective-permute-done.11 = bf16[1,64,768]{2,1,0:T(8,128)(2,1)S(1)} collective-permute-done((bf16[1,64,768]{2,1,0:T(8,128)(2,1)S(1)}, bf16[1,64,768]{2,1,0:T(8,128)(2,1)S(1)}, u32[]{:S(2)}, u32[]{:S(2)}) %collective-permute-start.11) | collective-permute-done | bytes 98336 | tf_op jit(solution)/shard_map/ppermute | solution.py:397
  65.9 13.9 %shard_map.165 = (bf16[4,128,768]{2,1,0:T(8,128)(2,1)}, f32[864,768]{1,0:T(8,128)}, bf16[864,768]{1,0:T(8,128)(2,1)}, bf16[864,768]{1,0:T(8,128)(2,1)}, f32[128,768]{1,0:T(8,128)}, /*index=5*/f32[128,768]{1,0:T(8,128)}) custom-call(s32[2]{0:T(128)} %pad_add_fusion.length_ref, f32[4,72,128]{2,1,0:T(8,128)} %copy.38.allow_ref, bf16[4,128,768]{2,1,0:T(8,128)(2,1)} %copy-done.3, ...), custom_call_target="tpu_custom_call" | custom-call | tf_op jit(solution)/shard_map/pallas_call | solution.py:278
  79.8 1.9 %collective-permute-start.13 = (bf16[864,768]{1,0:T(8,128)(2,1)}, bf16[864,768]{1,0:T(8,128)(2,1)S(1)}, u32[]{:S(2)}, u32[]{:S(2)}) collective-permute-start(bf16[864,768]{1,0:T(8,128)(2,1)} %get-tuple-element.44), channel_id=1, source_target_pairs={{0,240},{4,244},{8,248},{12,252},{16,224},{20,228},{24,232},{28,23... | collective-permute-start | bytes 3981320 | tf_op jit(solution)/shard_map/ppermute | solution.py:392
  82.7 3.5 %all-to-all-start.2 = ((bf16[4,128,768]{2,1,0:T(8,128)(2,1)}), bf16[4,128,768]{2,1,0:T(8,128)(2,1)S(1)}, u32[]{:S(2)}, u32[]{:S(2)}) async-start(bf16[4,128,768]{2,1,0:T(8,128)(2,1)} %get-tuple-element.40), calls=%async_computation.2 | async-start | bytes 1572864 | tf_op jit(solution)/shard_map/all_to_all | solution.py:403
  88.2 10.8 %all-to-all-done.2.packed_ref = bf16[4,128,768]{2,1,0:T(8,128)(2,1)S(1)} async-done(((bf16[4,128,768]{2,1,0:T(8,128)(2,1)}), bf16[4,128,768]{2,1,0:T(8,128)(2,1)S(1)}, u32[]{:S(2)}, u32[]{:S(2)}) %all-to-all-start.2) | async-done | bytes 786464 | tf_op jit(solution)/shard_map/all_to_all | solution.py:403
  100.4 2.2 %fusion.10 = (bf16[352,768]{1,0:T(8,128)(2,1)S(1)}, f32[352,768]{1,0:T(8,128)S(1)}) fusion(bf16[864,768]{1,0:T(8,128)(2,1)S(1)} %collective-permute-done.14.second_ref, bf16[864,768]{1,0:T(8,128)(2,1)S(1)} %collective-permute-done.13.first_ref, f32[864,768]{1,0:T(8,128)} %get-tuple-element.43.own_ref), kind=kLoop, calls=%fused_computation.58 | loop fusion | flops 1351680 | bytes 3784704 | tf_op jit(solution)/shard_map/convert.5
  103.7 2.4 %collective-permute-start.16 = (bf16[144,768]{1,0:T(8,128)(2,1)S(1)}, bf16[144,768]{1,0:T(8,128)(2,1)S(1)}, u32[]{:S(2)}, u32[]{:S(2)}) collective-permute-start(bf16[144,768]{1,0:T(8,128)(2,1)S(1)} %get-tuple-element.67), channel_id=1, source_target_pairs={{0,3},{1,0},{2,1},{3,2},{4,7},{5,4},{6,5},{7,6},{8,11},{9,8},{10,9... | collective-permute-start | bytes 663560 | tf_op jit(solution)/shard_map/ppermute | solution.py:379
  107.7 3.5 %collective-permute-done.15.left_ref = bf16[144,768]{1,0:T(8,128)(2,1)S(1)} collective-permute-done((bf16[144,768]{1,0:T(8,128)(2,1)S(1)}, bf16[144,768]{1,0:T(8,128)(2,1)S(1)}, u32[]{:S(2)}, u32[]{:S(2)}) %collective-permute-start.15) | collective-permute-done | bytes 221216 | tf_op jit(solution)/shard_map/ppermute | solution.py:379
  111.3 5.6 %collective-permute-start.17 = (bf16[64,768]{1,0:T(8,128)(2,1)S(1)}, bf16[64,768]{1,0:T(8,128)(2,1)S(1)}, u32[]{:S(2)}, u32[]{:S(2)}) collective-permute-start(bf16[64,768]{1,0:T(8,128)(2,1)S(1)} %pad_maximum_fusion.5), channel_id=1, source_target_pairs={{0,16},{4,20},{8,24},{12,28},{16,0},{20,4},{24,8},{28,12},{1,17},{... | collective-permute-start | bytes 294920 | tf_op jit(solution)/shard_map/ppermute | solution.py:397
  117.6 5.0 %collective-permute-done.22 = f32[2,8,768]{2,1,0:T(8,128)S(1)} collective-permute-done((f32[2,8,768]{2,1,0:T(8,128)S(1)}, f32[2,8,768]{2,1,0:T(8,128)S(1)}, u32[]{:S(2)}, u32[]{:S(2)}) %collective-permute-start.22) | collective-permute-done | bytes 49184 | tf_op jit(solution)/shard_map/ppermute | solution.py:397
  122.6 1.7 %collective-permute-start.23 = (f32[4,4,768]{2,1,0:T(4,128)S(1)}, f32[4,4,768]{2,1,0:T(4,128)S(1)}, u32[]{:S(2)}, u32[]{:S(2)}) collective-permute-start(f32[4,4,768]{2,1,0:T(4,128)S(1)} %get-tuple-element.72), channel_id=1, source_target_pairs={{0,64},{32,96},{64,0},{96,32},{128,192},{160,224},{192,128},{224,1... | collective-permute-start | bytes 147464 | tf_op jit(solution)/shard_map/ppermute | solution.py:397
  124.4 2.9 %shard_map.167 = bf16[4,128,768]{2,1,0:T(8,128)(2,1)} custom-call(s32[1]{0:T(128)} %bitcast.18.half_ref, f32[864,768]{1,0:T(8,128)} %get-tuple-element.43.own_ref, bf16[864,768]{1,0:T(8,128)(2,1)} %copy-done.4, bf16[864,768]{1,0:T(8,128)(2,1)} %copy-done.5, bf16[64,768]{1,0:T(8,128)(2,1)} %copy-done.10, bf16[144,768]{1,0:T(8,128)(2,1)} %copy-done.7, ...), custom_call_target="tpu_custom_call" | custom-call | tf_op jit(solution)/shard_map/pallas_call | solution.py:331
  127.3 2.8 %collective-permute-start.24 = (f32[4,2,768]{2,1,0:T(2,128)S(1)}, f32[4,2,768]{2,1,0:T(2,128)S(1)}, u32[]{:S(2)}, u32[]{:S(2)}) collective-permute-start(f32[4,2,768]{2,1,0:T(2,128)S(1)} %slice.193), channel_id=1, source_target_pairs={{0,128},{32,160},{64,192},{96,224},{128,0},{160,32},{192,64},{224,... | collective-permute-start | bytes 73736 | tf_op jit(solution)/shard_map/ppermute | solution.py:397
  130.1 3.5 %all-to-all-start.3 = ((bf16[4,128,768]{2,1,0:T(8,128)(2,1)}), bf16[4,128,768]{2,1,0:T(8,128)(2,1)S(1)}, u32[]{:S(2)}, u32[]{:S(2)}) async-start(bf16[4,128,768]{2,1,0:T(8,128)(2,1)} %shard_map.167), calls=%async_computation.3 | async-start | bytes 1572864 | tf_op jit(solution)/shard_map/all_to_all | solution.py:403
  133.7 2.3 %collective-permute-start.25 = (f32[4,1,768]{2,1,0:T(1,128)S(1)}, f32[4,1,768]{2,1,0:T(1,128)S(1)}, u32[]{:S(2)}, u32[]{:S(2)}) collective-permute-start(f32[4,1,768]{2,1,0:T(1,128)S(1)} %slice.195), channel_id=1, source_target_pairs={{0,16},{4,20},{8,24},{12,28},{16,0},{20,4},{24,8},{28,12},{1,17},{... | collective-permute-start | bytes 36872 | tf_op jit(solution)/shard_map/ppermute | solution.py:397
  136.0 2.3 %shard_map.166 = (bf16[128,1536]{1,0:T(8,128)(2,1)}, bf16[128,1536]{1,0:T(8,128)(2,1)}) custom-call(bf16[4,128,768]{2,1,0:T(8,128)(2,1)} %copy-done.1), custom_call_target="tpu_custom_call" | custom-call | tf_op jit(solution)/shard_map/pallas_call | solution.py:106
  138.2 3.2 %collective-permute-done.25 = f32[4,1,768]{2,1,0:T(1,128)S(1)} collective-permute-done((f32[4,1,768]{2,1,0:T(1,128)S(1)}, f32[4,1,768]{2,1,0:T(1,128)S(1)}, u32[]{:S(2)}, u32[]{:S(2)}) %collective-permute-start.25) | collective-permute-done | bytes 12320 | tf_op jit(solution)/shard_map/ppermute | solution.py:397
  144.0 2.3 %shard_map.168 = (bf16[128,1536]{1,0:T(8,128)(2,1)}, bf16[128,1536]{1,0:T(8,128)(2,1)}) custom-call(bf16[4,128,768]{2,1,0:T(8,128)(2,1)} %copy-done.2), custom_call_target="tpu_custom_call" | custom-call | tf_op jit(solution)/shard_map/pallas_call | solution.py:106
  (121 shorter events, 19.3 us)
Async XLA Ops:
  3.0 18.0 %all-to-all-start = ((bf16[4,144,768]{2,1,0:T(8,128)(2,1)}), bf16[4,144,768]{2,1,0:T(8,128)(2,1)S(1)}, u32[]{:S(2)}, u32[]{:S(2)}) async-start(bf16[4,144,768]{2,1,0:T(8,128)(2,1)} %shard_map.163), calls=%async_computation | async-start | bytes 1769472 | tf_op jit(solution)/shard_map/all_to_all | solution.py:403
  7.5 8.1 %collective-permute-start.3 = (bf16[4,1,768]{2,1,0:T(2,128)(2,1)S(1)}, bf16[4,1,768]{2,1,0:T(2,128)(2,1)S(1)}, u32[]{:S(2)}, u32[]{:S(2)}) collective-permute-start(bf16[4,1,768]{2,1,0:T(2,128)(2,1)S(1)} %copy.37), channel_id=1, source_target_pairs={{0,16},{4,20},{8,24},{12,28},{16,0},{20,4},{24,8},{28,12},{1,17},{... | collective-permute-start | bytes 18440 | tf_op jit(solution)/shard_map/ppermute | solution.py:397
  15.6 5.3 %collective-permute-start.4 = (bf16[4,2,768]{2,1,0:T(2,128)(2,1)S(1)}, bf16[4,2,768]{2,1,0:T(2,128)(2,1)S(1)}, u32[]{:S(2)}, u32[]{:S(2)}) collective-permute-start(bf16[4,2,768]{2,1,0:T(2,128)(2,1)S(1)} %pad_maximum_fusion.12), channel_id=1, source_target_pairs={{0,128},{32,160},{64,192},{96,224},{128,0},{160,32},{192,64},{224,... | collective-permute-start | bytes 36872 | tf_op jit(solution)/shard_map/ppermute | solution.py:397
  20.9 7.4 %collective-permute-start.5 = (bf16[4,4,768]{2,1,0:T(4,128)(2,1)S(1)}, bf16[4,4,768]{2,1,0:T(4,128)(2,1)S(1)}, u32[]{:S(2)}, u32[]{:S(2)}) collective-permute-start(bf16[4,4,768]{2,1,0:T(4,128)(2,1)S(1)} %pad_maximum_fusion.11), channel_id=1, source_target_pairs={{0,64},{32,96},{64,0},{96,32},{128,192},{160,224},{192,128},{224,1... | collective-permute-start | bytes 73736 | tf_op jit(solution)/shard_map/ppermute | solution.py:397
  21.5 16.3 %copy-start.13 = (s32[4,24]{1,0:T(4,128)S(1)}, s32[4,24]{1,0:T(4,128)}, u32[]{:S(2)}) copy-start(s32[4,24]{1,0:T(4,128)} %constant.53.clone) | copy-start | bytes 1156
  21.6 9.7 %collective-permute-start = (bf16[64,768]{1,0:T(8,128)(2,1)S(1)}, bf16[64,768]{1,0:T(8,128)(2,1)S(1)}, u32[]{:S(2)}, u32[]{:S(2)}) collective-permute-start(bf16[64,768]{1,0:T(8,128)(2,1)S(1)} %bitcast.40), channel_id=1, source_target_pairs={{0,16},{4,20},{8,24},{12,28},{16,0},{20,4},{24,8},{28,12},{1,17},{... | collective-permute-start | bytes 294920 | tf_op jit(solution)/shard_map/ppermute | solution.py:397
  31.3 5.6 %collective-permute-start.6 = (bf16[2,8,768]{2,1,0:T(8,128)(2,1)S(1)}, bf16[2,8,768]{2,1,0:T(8,128)(2,1)S(1)}, u32[]{:S(2)}, u32[]{:S(2)}) collective-permute-start(bf16[2,8,768]{2,1,0:T(8,128)(2,1)S(1)} %get-tuple-element.87), channel_id=1, source_target_pairs={{0,8},{4,12},{8,0},{12,4},{16,24},{20,28},{24,16},{28,20},{1,9},{5... | collective-permute-start | bytes 73736 | tf_op jit(solution)/shard_map/ppermute | solution.py:397
  33.9 6.9 %collective-permute-start.2 = (bf16[144,768]{1,0:T(8,128)(2,1)S(1)}, bf16[144,768]{1,0:T(8,128)(2,1)S(1)}, u32[]{:S(2)}, u32[]{:S(2)}) collective-permute-start(bf16[144,768]{1,0:T(8,128)(2,1)S(1)} %pad_maximum_fusion.2), channel_id=1, source_target_pairs={{0,3},{1,0},{2,1},{3,2},{4,7},{5,4},{6,5},{7,6},{8,11},{9,8},{10,9... | collective-permute-start | bytes 663560 | tf_op jit(solution)/shard_map/ppermute | solution.py:379
  36.7 7.2 %collective-permute-start.1 = (bf16[144,768]{1,0:T(8,128)(2,1)S(1)}, bf16[144,768]{1,0:T(8,128)(2,1)S(1)}, u32[]{:S(2)}, u32[]{:S(2)}) collective-permute-start(bf16[144,768]{1,0:T(8,128)(2,1)S(1)} %pad_maximum_fusion.1), channel_id=1, source_target_pairs={{0,1},{1,2},{2,3},{3,0},{4,5},{5,6},{6,7},{7,4},{8,9},{9,10},{10,1... | collective-permute-start | bytes 663560 | tf_op jit(solution)/shard_map/ppermute | solution.py:379
  36.9 3.9 %collective-permute-start.7 = (bf16[1,16,768]{2,1,0:T(8,128)(2,1)S(1)}, bf16[1,16,768]{2,1,0:T(8,128)(2,1)S(1)}, u32[]{:S(2)}, u32[]{:S(2)}) collective-permute-start(bf16[1,16,768]{2,1,0:T(8,128)(2,1)S(1)} %get-tuple-element.85), channel_id=1, source_target_pairs={{0,4},{4,0},{8,12},{12,8},{16,20},{20,16},{24,28},{28,24},{1,5},{5... | collective-permute-start | bytes 73736 | tf_op jit(solution)/shard_map/ppermute | solution.py:397
  44.9 17.0 %copy-start = (bf16[864,768]{1,0:T(8,128)(2,1)}, bf16[864,768]{1,0:T(8,128)(2,1)S(1)}, u32[]{:S(2)}) copy-start(bf16[864,768]{1,0:T(8,128)(2,1)S(1)} %pad_maximum_fusion.here_ref) | copy-start | bytes 3981316
  45.0 20.9 %collective-permute-start.9 = (bf16[864,768]{1,0:T(8,128)(2,1)S(1)}, bf16[864,768]{1,0:T(8,128)(2,1)}, u32[]{:S(2)}, u32[]{:S(2)}) collective-permute-start(bf16[864,768]{1,0:T(8,128)(2,1)S(1)} %pad_maximum_fusion.here_ref), channel_id=1, source_target_pairs={{0,240},{4,244},{8,248},{12,252},{16,224},{20,228},{24,232},{28,23... | collective-permute-start | bytes 3981320 | tf_op jit(solution)/shard_map/ppermute | solution.py:392
  45.0 20.9 %collective-permute-start.8 = (bf16[864,768]{1,0:T(8,128)(2,1)S(1)}, bf16[864,768]{1,0:T(8,128)(2,1)}, u32[]{:S(2)}, u32[]{:S(2)}) collective-permute-start(bf16[864,768]{1,0:T(8,128)(2,1)S(1)} %pad_maximum_fusion.here_ref), channel_id=1, source_target_pairs={{0,32},{4,36},{8,40},{12,44},{16,48},{20,52},{24,56},{28,60},{32,6... | collective-permute-start | bytes 3981320 | tf_op jit(solution)/shard_map/ppermute | solution.py:392
  47.0 15.9 %all-to-all-start.1 = ((bf16[4,128,768]{2,1,0:T(8,128)(2,1)}), bf16[4,128,768]{2,1,0:T(8,128)(2,1)S(1)}, u32[]{:S(2)}, u32[]{:S(2)}) async-start(bf16[4,128,768]{2,1,0:T(8,128)(2,1)} %shard_map.164), calls=%async_computation.1 | async-start | bytes 1572864 | tf_op jit(solution)/shard_map/all_to_all | solution.py:403
  50.5 5.7 %collective-permute-start.10 = (bf16[1,32,768]{2,1,0:T(8,128)(2,1)S(1)}, bf16[1,32,768]{2,1,0:T(8,128)(2,1)S(1)}, u32[]{:S(2)}, u32[]{:S(2)}) collective-permute-start(bf16[1,32,768]{2,1,0:T(8,128)(2,1)S(1)} %pad_maximum_fusion.9), channel_id=1, source_target_pairs={{0,2},{1,3},{2,0},{3,1},{4,6},{5,7},{6,4},{7,5},{8,10},{9,11},{10,... | collective-permute-start | bytes 147464 | tf_op jit(solution)/shard_map/ppermute | solution.py:397
  56.2 5.7 %collective-permute-start.11 = (bf16[1,64,768]{2,1,0:T(8,128)(2,1)S(1)}, bf16[1,64,768]{2,1,0:T(8,128)(2,1)S(1)}, u32[]{:S(2)}, u32[]{:S(2)}) collective-permute-start(bf16[1,64,768]{2,1,0:T(8,128)(2,1)S(1)} %pad_maximum_fusion.4), channel_id=1, source_target_pairs={{0,1},{1,0},{2,3},{3,2},{4,5},{5,4},{6,7},{7,6},{8,9},{9,8},{10,11... | collective-permute-start | bytes 294920 | tf_op jit(solution)/shard_map/ppermute | solution.py:397
  63.0 2.1 %collective-permute-start.12 = (bf16[1,128,768]{2,1,0:T(8,128)(2,1)S(1)}, bf16[1,128,768]{2,1,0:T(8,128)(2,1)S(1)}, u32[]{:S(2)}, u32[]{:S(2)}) collective-permute-start(bf16[1,128,768]{2,1,0:T(8,128)(2,1)S(1)} %pad_maximum_fusion.3), channel_id=1, source_target_pairs={{0,32},{32,0},{64,96},{96,64},{128,160},{160,128},{192,224},{224,1... | collective-permute-start | bytes 589832 | tf_op jit(solution)/shard_map/ppermute | solution.py:397
  79.8 20.6 %collective-permute-start.13 = (bf16[864,768]{1,0:T(8,128)(2,1)}, bf16[864,768]{1,0:T(8,128)(2,1)S(1)}, u32[]{:S(2)}, u32[]{:S(2)}) collective-permute-start(bf16[864,768]{1,0:T(8,128)(2,1)} %get-tuple-element.44), channel_id=1, source_target_pairs={{0,240},{4,244},{8,248},{12,252},{16,224},{20,228},{24,232},{28,23... | collective-permute-start | bytes 3981320 | tf_op jit(solution)/shard_map/ppermute | solution.py:392
  81.7 18.7 %collective-permute-start.14 = (bf16[864,768]{1,0:T(8,128)(2,1)}, bf16[864,768]{1,0:T(8,128)(2,1)S(1)}, u32[]{:S(2)}, u32[]{:S(2)}) collective-permute-start(bf16[864,768]{1,0:T(8,128)(2,1)} %get-tuple-element.45), channel_id=1, source_target_pairs={{0,32},{4,36},{8,40},{12,44},{16,48},{20,52},{24,56},{28,60},{32,6... | collective-permute-start | bytes 3981320 | tf_op jit(solution)/shard_map/ppermute | solution.py:392
  81.7 4.5 %collective-permute-start.18 = (f32[1,128,768]{2,1,0:T(8,128)}, f32[1,128,768]{2,1,0:T(8,128)}, u32[]{:S(2)}, u32[]{:S(2)}) collective-permute-start(f32[1,128,768]{2,1,0:T(8,128)} %bitcast.46), channel_id=1, source_target_pairs={{0,32},{32,0},{64,96},{96,64},{128,160},{160,128},{192,224},{224,1... | collective-permute-start | bytes 1179656 | tf_op jit(solution)/shard_map/ppermute | solution.py:397
  82.7 16.2 %all-to-all-start.2 = ((bf16[4,128,768]{2,1,0:T(8,128)(2,1)}), bf16[4,128,768]{2,1,0:T(8,128)(2,1)S(1)}, u32[]{:S(2)}, u32[]{:S(2)}) async-start(bf16[4,128,768]{2,1,0:T(8,128)(2,1)} %get-tuple-element.40), calls=%async_computation.2 | async-start | bytes 1572864 | tf_op jit(solution)/shard_map/all_to_all | solution.py:403
  88.2 10.8 %collective-permute-start.19 = (f32[1,64,768]{2,1,0:T(8,128)}, f32[1,64,768]{2,1,0:T(8,128)}, u32[]{:S(2)}, u32[]{:S(2)}) collective-permute-start(f32[1,64,768]{2,1,0:T(8,128)} %get-tuple-element.68), channel_id=1, source_target_pairs={{0,1},{1,0},{2,3},{3,2},{4,5},{5,4},{6,7},{7,6},{8,9},{9,8},{10,11... | collective-permute-start | bytes 589832 | tf_op jit(solution)/shard_map/ppermute | solution.py:397
  100.3 6.7 %collective-permute-start.20 = (f32[1,32,768]{2,1,0:T(8,128)S(1)}, f32[1,32,768]{2,1,0:T(8,128)S(1)}, u32[]{:S(2)}, u32[]{:S(2)}) collective-permute-start(f32[1,32,768]{2,1,0:T(8,128)S(1)} %get-tuple-element.70), channel_id=1, source_target_pairs={{0,2},{1,3},{2,0},{3,1},{4,6},{5,7},{6,4},{7,5},{8,10},{9,11},{10,... | collective-permute-start | bytes 294920 | tf_op jit(solution)/shard_map/ppermute | solution.py:397
  102.7 8.5 %collective-permute-start.15 = (bf16[144,768]{1,0:T(8,128)(2,1)S(1)}, bf16[144,768]{1,0:T(8,128)(2,1)S(1)}, u32[]{:S(2)}, u32[]{:S(2)}) collective-permute-start(bf16[144,768]{1,0:T(8,128)(2,1)S(1)} %get-tuple-element.66), channel_id=1, source_target_pairs={{0,1},{1,2},{2,3},{3,0},{4,5},{5,6},{6,7},{7,4},{8,9},{9,10},{10,1... | collective-permute-start | bytes 663560 | tf_op jit(solution)/shard_map/ppermute | solution.py:379
  103.7 7.5 %collective-permute-start.16 = (bf16[144,768]{1,0:T(8,128)(2,1)S(1)}, bf16[144,768]{1,0:T(8,128)(2,1)S(1)}, u32[]{:S(2)}, u32[]{:S(2)}) collective-permute-start(bf16[144,768]{1,0:T(8,128)(2,1)S(1)} %get-tuple-element.67), channel_id=1, source_target_pairs={{0,3},{1,0},{2,1},{3,2},{4,7},{5,4},{6,5},{7,6},{8,11},{9,8},{10,9... | collective-permute-start | bytes 663560 | tf_op jit(solution)/shard_map/ppermute | solution.py:379
  107.0 9.9 %collective-permute-start.21 = (f32[1,16,768]{2,1,0:T(8,128)S(1)}, f32[1,16,768]{2,1,0:T(8,128)S(1)}, u32[]{:S(2)}, u32[]{:S(2)}) collective-permute-start(f32[1,16,768]{2,1,0:T(8,128)S(1)} %get-tuple-element.80), channel_id=1, source_target_pairs={{0,4},{4,0},{8,12},{12,8},{16,20},{20,16},{24,28},{28,24},{1,5},{5... | collective-permute-start | bytes 147464 | tf_op jit(solution)/shard_map/ppermute | solution.py:397
  111.3 11.3 %collective-permute-start.17 = (bf16[64,768]{1,0:T(8,128)(2,1)S(1)}, bf16[64,768]{1,0:T(8,128)(2,1)S(1)}, u32[]{:S(2)}, u32[]{:S(2)}) collective-permute-start(bf16[64,768]{1,0:T(8,128)(2,1)S(1)} %pad_maximum_fusion.5), channel_id=1, source_target_pairs={{0,16},{4,20},{8,24},{12,28},{16,0},{20,4},{24,8},{28,12},{1,17},{... | collective-permute-start | bytes 294920 | tf_op jit(solution)/shard_map/ppermute | solution.py:397
  116.9 5.7 %collective-permute-start.22 = (f32[2,8,768]{2,1,0:T(8,128)S(1)}, f32[2,8,768]{2,1,0:T(8,128)S(1)}, u32[]{:S(2)}, u32[]{:S(2)}) collective-permute-start(f32[2,8,768]{2,1,0:T(8,128)S(1)} %get-tuple-element.76), channel_id=1, source_target_pairs={{0,8},{4,12},{8,0},{12,4},{16,24},{20,28},{24,16},{28,20},{1,9},{5... | collective-permute-start | bytes 147464 | tf_op jit(solution)/shard_map/ppermute | solution.py:397
  122.6 4.7 %collective-permute-start.23 = (f32[4,4,768]{2,1,0:T(4,128)S(1)}, f32[4,4,768]{2,1,0:T(4,128)S(1)}, u32[]{:S(2)}, u32[]{:S(2)}) collective-permute-start(f32[4,4,768]{2,1,0:T(4,128)S(1)} %get-tuple-element.72), channel_id=1, source_target_pairs={{0,64},{32,96},{64,0},{96,32},{128,192},{160,224},{192,128},{224,1... | collective-permute-start | bytes 147464 | tf_op jit(solution)/shard_map/ppermute | solution.py:397
  127.3 6.3 %collective-permute-start.24 = (f32[4,2,768]{2,1,0:T(2,128)S(1)}, f32[4,2,768]{2,1,0:T(2,128)S(1)}, u32[]{:S(2)}, u32[]{:S(2)}) collective-permute-start(f32[4,2,768]{2,1,0:T(2,128)S(1)} %slice.193), channel_id=1, source_target_pairs={{0,128},{32,160},{64,192},{96,224},{128,0},{160,32},{192,64},{224,... | collective-permute-start | bytes 73736 | tf_op jit(solution)/shard_map/ppermute | solution.py:397
  130.1 13.0 %all-to-all-start.3 = ((bf16[4,128,768]{2,1,0:T(8,128)(2,1)}), bf16[4,128,768]{2,1,0:T(8,128)(2,1)S(1)}, u32[]{:S(2)}, u32[]{:S(2)}) async-start(bf16[4,128,768]{2,1,0:T(8,128)(2,1)} %shard_map.167), calls=%async_computation.3 | async-start | bytes 1572864 | tf_op jit(solution)/shard_map/all_to_all | solution.py:403
  133.7 7.7 %collective-permute-start.25 = (f32[4,1,768]{2,1,0:T(1,128)S(1)}, f32[4,1,768]{2,1,0:T(1,128)S(1)}, u32[]{:S(2)}, u32[]{:S(2)}) collective-permute-start(f32[4,1,768]{2,1,0:T(1,128)S(1)} %slice.195), channel_id=1, source_target_pairs={{0,16},{4,20},{8,24},{12,28},{16,0},{20,4},{24,8},{28,12},{1,17},{... | collective-permute-start | bytes 36872 | tf_op jit(solution)/shard_map/ppermute | solution.py:397
  (14 other events, 85.5 us)

commit v2 on v1

--- a/solution.py
+++ b/solution.py
@@ -139,8 +139,10 @@
     text_ref,
     od_ref,
     here_out,
-    below_out,
-    above_out,
+    own_below_out,
+    own_above_out,
+    halo_below_out,
+    halo_above_out,
     text_out,
     text_away_out,
     below_sum,
@@ -257,8 +259,10 @@
     lane = lax.broadcasted_iota(jnp.int32, (1, PAIR), 1)
     factor = jnp.where(lane < HEAD, scale, 1.0).astype(F32)
     here_out[...] = here_out[...] * factor
-    below_out[...] = (below_sum[...] * factor).astype(BF16)
-    above_out[...] = (above_sum[...] * factor).astype(BF16)
+    own_below_out[...] = (below_sum[:OWN, :] * factor).astype(BF16)
+    own_above_out[...] = (above_sum[:OWN, :] * factor).astype(BF16)
+    halo_below_out[...] = (below_sum[OWN:, :] * factor).astype(BF16)
+    halo_above_out[...] = (above_sum[OWN:, :] * factor).astype(BF16)
     text_out[...] = text_out[...] * factor
     text_away_out[...] = text_away_out[...] * factor
 
@@ -285,12 +289,17 @@
         ]
         + [spec(ALL)] * 3
         + [spec(text_count)],
-        out_specs=[part] + [spec(ALL)] * 3 + [spec(text_count // 2)] * 2,
+        out_specs=[part, spec(ALL)]
+        + [spec(OWN)] * 2
+        + [spec(ALL - OWN)] * 2
+        + [spec(text_count // 2)] * 2,
         out_shape=[
             jax.ShapeDtypeStruct(qg.shape, BF16),
             shape(ALL, F32),
-            shape(ALL, BF16),
-            shape(ALL, BF16),
+            shape(OWN, BF16),
+            shape(OWN, BF16),
+            shape(ALL - OWN, BF16),
+            shape(ALL - OWN, BF16),
             shape(text_count // 2, F32),
             shape(text_count // 2, F32),
         ],
@@ -502,7 +511,7 @@
 
     me = (lax.axis_index("ta") * lax.axis_size("ha") + lax.axis_index("ha")) * lax.axis_size("wa")
     me = me + lax.axis_index("wa")
-    od, here_grad, below_grad, above_grad, text_grad, text_away = attention(
+    od, here_grad, own_below, own_above, halo_below, halo_above, text_grad, text_away = attention(
         jnp.concatenate([text_length, me.reshape(1)]),
         allow,
         qg,
@@ -513,21 +522,22 @@
         text_bits(),
     )
 
-    first = turned_time(below_grad, -1)
-    second = turned_time(above_grad, 1)
+    halo_first = turned_time(halo_below, -1)
+    halo_second = turned_time(halo_above, 1)
+    first = turned_time(after(own_below, halo_first, halo_second), -1)
+    second = turned_time(after(own_above, halo_first, halo_second), 1)
     back = steps[::-1]
     text_grad = sent_text(text_grad[None], text_away[None], *back[0])
     text_grad = scatter_text(text_grad, *back[1])
     od_in = regrouped(od)
-    text_grad = scatter_text(text_grad, *back[2], od_in)
-    halo = here_grad[OWN:] + first[OWN:].astype(F32) + second[OWN:].astype(F32)
+    halo = here_grad[OWN:] + halo_first.astype(F32) + halo_second.astype(F32)
     side = SIDE + TILE
     to_left = halo[:side].astype(BF16)
     to_right = halo[side : 2 * side].astype(BF16)
     rim_grad = halo[2 * side :]
     right = turned_width(to_left, -1)
     left = turned_width(to_right, 1)
-    text_grad = scatter_text(text_grad, *back[3], to_left, to_right)
+    text_grad = scatter_text(text_grad, *back[2], to_left, to_right)
     rim_out = jnp.concatenate(
         [
             rim_grad[:TILE] + left[SIDE:].astype(F32),
@@ -537,11 +547,13 @@
         0,
     ).astype(BF16)
     rim_in = swapped(rim_out, "ha", GROUP)
-    text_grad = scatter_text(text_grad, *back[4], rim_out)
-    text_grad = scatter_text(text_grad, *back[5], rim_in)
+    text_grad = scatter_text(text_grad, *back[3], rim_out)
+    text_grad = scatter_text(text_grad, *back[4], rim_in, first, second)
     grads = settle(half.reshape(1), here_grad, first, second, rim_in, left, right)
-    text_grad = scatter_text(text_grad, *back[6], grads)
-    text_grad = joined_text(scatter_text(text_grad, *back[7]))
+    text_grad = scatter_text(text_grad, *back[5], grads)
+    for step in back[6:]:
+        text_grad = scatter_text(text_grad, *step)
+    text_grad = joined_text(text_grad)
     attended, query_grad = unpack(od_in)
     key_grad, value_grad = unpack(regrouped(grads))
     text_grad = text_grad.astype(BF16).reshape(-1, 2, HEAD)

time: 147 us -> 152 us (1.034)
  waiting for transfers between devices: 47.3 us -> 52 us
  starting transfers between devices: 59.7 us -> 62.8 us
  other arithmetic: 7.85 us -> 5.64 us
    ppermute x4 -> x6, waiting for transfers between devices: 0.01 us -> 7.81 us  [turned_time(): return lax.ppermute(value, ('ta', 'ha'), pairs)]
    all_to_all x4, waiting for transfers between devices: 12.8 us -> 7.72 us  [regrouped(): return lax.all_to_all(value, 'ha', 0, 0, axis_index_groups=groups)]
    ppermute x4, waiting for transfers between devices: 6.7 us -> 10.9 us  [turned_width(): lax.ppermute(value, 'wa', [(i, (i + step) % count) for i in range(count)])]
    ppermute x18, starting transfers between devices: 36.1 us -> 38.7 us  [swapped(): return lax.ppermute(value, axis, [(i, i ^ bit) for i in range(count)])]
    ppermute x18, waiting for transfers between devices: 27.7 us -> 25.5 us  [swapped(): return lax.ppermute(value, axis, [(i, i ^ bit) for i in range(count)])]
  transfers between devices with their start and end apart: 30 -> 32, of which waited for: 14 -> 17; matrix products, arithmetic and copies ran while one was open for 6% -> 4% of each run, Pallas kernels for 5% -> 5%
where the time goes in v2:
time: 152 us; the launch traced here: 151 us
  starting transfers between devices  62.8 us (41%)
  waiting for transfers between devices  52 us (34%)
  Pallas kernels  26 us (17%)
  other arithmetic  5.64 us (4%)
  local copies, waits for them, and re-layouts  2.97 us (2%)
  between operations  1.77 us (1%)
    ppermute x18, starting transfers between devices, swapped(): return lax.ppermute(value, axis, [(i, i ^ bit) for i in range(count)])  38.7 us
    ppermute x18, waiting for transfers between devices, swapped(): return lax.ppermute(value, axis, [(i, i ^ bit) for i in range(count)])  25.5 us
    all_to_all x4, starting transfers between devices, regrouped(): return lax.all_to_all(value, 'ha', 0, 0, axis_index_groups=groups)  14.9 us
    pallas_call x1, Pallas kernels, attention(): pl.pallas_call(functools.partial(attention_kernel, text_bits), grid=(head...  13.9 us
    ppermute x4, waiting for transfers between devices, turned_width(): lax.ppermute(value, 'wa', [(i, (i + step) % count) for i in range(count)])  10.9 us
    ppermute x6, waiting for transfers between devices, turned_time(): return lax.ppermute(value, ('ta', 'ha'), pairs)  7.81 us
    all_to_all x4, waiting for transfers between devices, regrouped(): return lax.all_to_all(value, 'ha', 0, 0, axis_index_groups=groups)  7.72 us
    ppermute x4, starting transfers between devices, turned_width(): lax.ppermute(value, 'wa', [(i, (i + step) % count) for i in range(count)])  6.22 us
  transfers between devices with their start and end apart: 32, of which 17 were waited for; matrix products, arithmetic and copies ran while one was open for 4% of the time, Pallas kernels for 5%

profile of v2, /device:TPU:32, one launch (start us, length us, event | category | flops | bytes accessed | tf_op | source)
XLA Modules:
  0.0 151.2 jit_solution(5925023980692658381)
XLA Ops:
  0.7 2.3 %shard_map.163 = bf16[4,144,768]{2,1,0:T(8,128)(2,1)} custom-call(bf16[128,1536]{1,0:T(8,128)(2,1)} %bitcast.36, bf16[128,1536]{1,0:T(8,128)(2,1)} %bitcast.37, s32[8,27]{1,0:T(8,128)} %bitcast.43), custom_call_target="tpu_custom_call" | custom-call | tf_op jit(solution)/shard_map/pallas_call | solution.py:78
  3.0 4.5 %all-to-all-start = ((bf16[4,144,768]{2,1,0:T(8,128)(2,1)}), bf16[4,144,768]{2,1,0:T(8,128)(2,1)S(1)}, u32[]{:S(2)}, u32[]{:S(2)}) async-start(bf16[4,144,768]{2,1,0:T(8,128)(2,1)} %shard_map.163), calls=%async_computation | async-start | bytes 1769472 | tf_op jit(solution)/shard_map/all_to_all | solution.py:412
  7.5 6.4 %collective-permute-start.3 = (bf16[4,1,768]{2,1,0:T(2,128)(2,1)S(1)}, bf16[4,1,768]{2,1,0:T(2,128)(2,1)S(1)}, u32[]{:S(2)}, u32[]{:S(2)}) collective-permute-start(bf16[4,1,768]{2,1,0:T(2,128)(2,1)S(1)} %copy.37), channel_id=1, source_target_pairs={{0,16},{4,20},{8,24},{12,28},{16,0},{20,4},{24,8},{28,12},{1,17},{... | collective-permute-start | bytes 18440 | tf_op jit(solution)/shard_map/ppermute | solution.py:406
  15.6 3.0 %collective-permute-start.4 = (bf16[4,2,768]{2,1,0:T(2,128)(2,1)S(1)}, bf16[4,2,768]{2,1,0:T(2,128)(2,1)S(1)}, u32[]{:S(2)}, u32[]{:S(2)}) collective-permute-start(bf16[4,2,768]{2,1,0:T(2,128)(2,1)S(1)} %pad_maximum_fusion.12), channel_id=1, source_target_pairs={{0,128},{32,160},{64,192},{96,224},{128,0},{160,32},{192,64},{224,... | collective-permute-start | bytes 36872 | tf_op jit(solution)/shard_map/ppermute | solution.py:406
  18.6 2.3 %shard_map.164 = bf16[4,128,768]{2,1,0:T(8,128)(2,1)} custom-call(bf16[128,1536]{1,0:T(8,128)(2,1)} %bitcast.38, bf16[128,1536]{1,0:T(8,128)(2,1)} %bitcast.39), custom_call_target="tpu_custom_call" | custom-call | tf_op jit(solution)/shard_map/pallas_call | solution.py:78
  21.6 6.7 %collective-permute-start = (bf16[64,768]{1,0:T(8,128)(2,1)S(1)}, bf16[64,768]{1,0:T(8,128)(2,1)S(1)}, u32[]{:S(2)}, u32[]{:S(2)}) collective-permute-start(bf16[64,768]{1,0:T(8,128)(2,1)S(1)} %bitcast.40), channel_id=1, source_target_pairs={{0,16},{4,20},{8,24},{12,28},{16,0},{20,4},{24,8},{28,12},{1,17},{... | collective-permute-start | bytes 294920 | tf_op jit(solution)/shard_map/ppermute | solution.py:406
  28.3 2.9 %collective-permute-done = bf16[64,768]{1,0:T(8,128)(2,1)S(1)} collective-permute-done((bf16[64,768]{1,0:T(8,128)(2,1)S(1)}, bf16[64,768]{1,0:T(8,128)(2,1)S(1)}, u32[]{:S(2)}, u32[]{:S(2)}) %collective-permute-start) | collective-permute-done | bytes 98336 | tf_op jit(solution)/shard_map/ppermute | solution.py:406
  31.2 2.6 %collective-permute-start.6 = (bf16[2,8,768]{2,1,0:T(8,128)(2,1)S(1)}, bf16[2,8,768]{2,1,0:T(8,128)(2,1)S(1)}, u32[]{:S(2)}, u32[]{:S(2)}) collective-permute-start(bf16[2,8,768]{2,1,0:T(8,128)(2,1)S(1)} %get-tuple-element.89), channel_id=1, source_target_pairs={{0,8},{4,12},{8,0},{12,4},{16,24},{20,28},{24,16},{28,20},{1,9},{5... | collective-permute-start | bytes 73736 | tf_op jit(solution)/shard_map/ppermute | solution.py:406
  33.9 2.8 %collective-permute-start.2 = (bf16[144,768]{1,0:T(8,128)(2,1)S(1)}, bf16[144,768]{1,0:T(8,128)(2,1)S(1)}, u32[]{:S(2)}, u32[]{:S(2)}) collective-permute-start(bf16[144,768]{1,0:T(8,128)(2,1)S(1)} %pad_maximum_fusion.2), channel_id=1, source_target_pairs={{0,3},{1,0},{2,1},{3,2},{4,7},{5,4},{6,5},{7,6},{8,11},{9,8},{10,9... | collective-permute-start | bytes 663560 | tf_op jit(solution)/shard_map/ppermute | solution.py:388
  37.8 3.0 %collective-permute-done.7 = bf16[1,16,768]{2,1,0:T(8,128)(2,1)S(1)} collective-permute-done((bf16[1,16,768]{2,1,0:T(8,128)(2,1)S(1)}, bf16[1,16,768]{2,1,0:T(8,128)(2,1)S(1)}, u32[]{:S(2)}, u32[]{:S(2)}) %collective-permute-start.7) | collective-permute-done | bytes 24608 | tf_op jit(solution)/shard_map/ppermute | solution.py:406
  40.8 3.2 %collective-permute-done.1 = bf16[144,768]{1,0:T(8,128)(2,1)S(1)} collective-permute-done((bf16[144,768]{1,0:T(8,128)(2,1)S(1)}, bf16[144,768]{1,0:T(8,128)(2,1)S(1)}, u32[]{:S(2)}, u32[]{:S(2)}) %collective-permute-start.1) | collective-permute-done | bytes 221216 | tf_op jit(solution)/shard_map/ppermute | solution.py:388
  47.0 3.5 %all-to-all-start.1 = ((bf16[4,128,768]{2,1,0:T(8,128)(2,1)}), bf16[4,128,768]{2,1,0:T(8,128)(2,1)S(1)}, u32[]{:S(2)}, u32[]{:S(2)}) async-start(bf16[4,128,768]{2,1,0:T(8,128)(2,1)} %shard_map.164), calls=%async_computation.1 | async-start | bytes 1572864 | tf_op jit(solution)/shard_map/all_to_all | solution.py:412
  50.6 5.6 %collective-permute-done.10 = bf16[1,32,768]{2,1,0:T(8,128)(2,1)S(1)} collective-permute-done((bf16[1,32,768]{2,1,0:T(8,128)(2,1)S(1)}, bf16[1,32,768]{2,1,0:T(8,128)(2,1)S(1)}, u32[]{:S(2)}, u32[]{:S(2)}) %collective-permute-start.10) | collective-permute-done | bytes 49184 | tf_op jit(solution)/shard_map/ppermute | solution.py:406
  56.8 5.1 %collective-permute-done.11 = bf16[1,64,768]{2,1,0:T(8,128)(2,1)S(1)} collective-permute-done((bf16[1,64,768]{2,1,0:T(8,128)(2,1)S(1)}, bf16[1,64,768]{2,1,0:T(8,128)(2,1)S(1)}, u32[]{:S(2)}, u32[]{:S(2)}) %collective-permute-start.11) | collective-permute-done | bytes 98336 | tf_op jit(solution)/shard_map/ppermute | solution.py:406
  65.8 13.9 %shard_map.165 = (bf16[4,128,768]{2,1,0:T(8,128)(2,1)}, f32[864,768]{1,0:T(8,128)}, bf16[512,768]{1,0:T(8,128)(2,1)}, bf16[512,768]{1,0:T(8,128)(2,1)}, bf16[352...) custom-call(s32[2]{0:T(128)} %pad_add_fusion.length_ref, ...), custom_call_target="tpu_custom_call" | custom-call | tf_op jit(solution)/shard_map/pallas_call | solution.py:282
  80.5 1.9 %collective-permute-start.13 = (bf16[352,768]{1,0:T(8,128)(2,1)}, bf16[352,768]{1,0:T(8,128)(2,1)S(1)}, u32[]{:S(2)}, u32[]{:S(2)}) collective-permute-start(bf16[352,768]{1,0:T(8,128)(2,1)} %get-tuple-element.47), channel_id=1, source_target_pairs={{0,240},{4,244},{8,248},{12,252},{16,224},{20,228},{24,232},{28,23... | collective-permute-start | bytes 1622024 | tf_op jit(solution)/shard_map/ppermute | solution.py:401
  83.6 6.0 %collective-permute-done.13 = bf16[352,768]{1,0:T(8,128)(2,1)S(1)} collective-permute-done((bf16[352,768]{1,0:T(8,128)(2,1)}, bf16[352,768]{1,0:T(8,128)(2,1)S(1)}, u32[]{:S(2)}, u32[]{:S(2)}) %collective-permute-start.13) | collective-permute-done | bytes 540704 | tf_op jit(solution)/shard_map/ppermute | solution.py:401
  89.6 1.8 %collective-permute-done.14 = bf16[352,768]{1,0:T(8,128)(2,1)S(1)} collective-permute-done((bf16[352,768]{1,0:T(8,128)(2,1)}, bf16[352,768]{1,0:T(8,128)(2,1)S(1)}, u32[]{:S(2)}, u32[]{:S(2)}) %collective-permute-start.14) | collective-permute-done | bytes 540704 | tf_op jit(solution)/shard_map/ppermute | solution.py:401
  93.5 3.2 %collective-permute-start.18 = (bf16[144,768]{1,0:T(8,128)(2,1)S(1)}, bf16[144,768]{1,0:T(8,128)(2,1)S(1)}, u32[]{:S(2)}, u32[]{:S(2)}) collective-permute-start(bf16[144,768]{1,0:T(8,128)(2,1)S(1)} %get-tuple-element.71), channel_id=1, source_target_pairs={{0,3},{1,0},{2,1},{3,2},{4,7},{5,4},{6,5},{7,6},{8,11},{9,8},{10,9... | collective-permute-start | bytes 663560 | tf_op jit(solution)/shard_map/ppermute | solution.py:388
  96.8 7.8 %collective-permute-done.17.left_ref = bf16[144,768]{1,0:T(8,128)(2,1)S(1)} collective-permute-done((bf16[144,768]{1,0:T(8,128)(2,1)S(1)}, bf16[144,768]{1,0:T(8,128)(2,1)S(1)}, u32[]{:S(2)}, u32[]{:S(2)}) %collective-permute-start.17) | collective-permute-done | bytes 221216 | tf_op jit(solution)/shard_map/ppermute | solution.py:388
  104.7 5.9 %collective-permute-start.19 = (bf16[64,768]{1,0:T(8,128)(2,1)S(1)}, bf16[64,768]{1,0:T(8,128)(2,1)S(1)}, u32[]{:S(2)}, u32[]{:S(2)}) collective-permute-start(bf16[64,768]{1,0:T(8,128)(2,1)S(1)} %pad_maximum_fusion.5), channel_id=1, source_target_pairs={{0,16},{4,20},{8,24},{12,28},{16,0},{20,4},{24,8},{28,12},{1,17},{... | collective-permute-start | bytes 294920 | tf_op jit(solution)/shard_map/ppermute | solution.py:406
  111.2 3.5 %collective-permute-done.23 = f32[1,16,768]{2,1,0:T(8,128)S(1)} collective-permute-done((f32[1,16,768]{2,1,0:T(8,128)S(1)}, f32[1,16,768]{2,1,0:T(8,128)S(1)}, u32[]{:S(2)}, u32[]{:S(2)}) %collective-permute-start.23) | collective-permute-done | bytes 49184 | tf_op jit(solution)/shard_map/ppermute | solution.py:406
  117.0 3.5 %all-to-all-start.2 = ((bf16[4,128,768]{2,1,0:T(8,128)(2,1)}), bf16[4,128,768]{2,1,0:T(8,128)(2,1)S(1)}, u32[]{:S(2)}, u32[]{:S(2)}) async-start(bf16[4,128,768]{2,1,0:T(8,128)(2,1)} %get-tuple-element.42), calls=%async_computation.2 | async-start | bytes 1572864 | tf_op jit(solution)/shard_map/all_to_all | solution.py:412
  120.5 2.9 %shard_map.167 = bf16[4,128,768]{2,1,0:T(8,128)(2,1)} custom-call(s32[1]{0:T(128)} %bitcast.18.half_ref, f32[864,768]{1,0:T(8,128)} %get-tuple-element.45.own_ref, bf16[512,768]{1,0:T(8,128)(2,1)} %copy-done.4, bf16[512,768]{1,0:T(8,128)(2,1)} %copy-done.5, bf16[64,768]{1,0:T(8,128)(2,1)} %copy-done.10, bf16[144,768]{1,0:T(8,128)(2,1)} %copy-done.7, ...), custom_call_target="tpu_custom_call" | custom-call | tf_op jit(solution)/shard_map/pallas_call | solution.py:340
  123.5 3.7 %collective-permute-start.25 = (f32[4,4,768]{2,1,0:T(4,128)S(1)}, f32[4,4,768]{2,1,0:T(4,128)S(1)}, u32[]{:S(2)}, u32[]{:S(2)}) collective-permute-start(f32[4,4,768]{2,1,0:T(4,128)S(1)} %pad_maximum_fusion.6), channel_id=1, source_target_pairs={{0,64},{32,96},{64,0},{96,32},{128,192},{160,224},{192,128},{224,1... | collective-permute-start | bytes 147464 | tf_op jit(solution)/shard_map/ppermute | solution.py:406
  127.2 2.1 %collective-permute-done.25 = f32[4,4,768]{2,1,0:T(4,128)S(1)} collective-permute-done((f32[4,4,768]{2,1,0:T(4,128)S(1)}, f32[4,4,768]{2,1,0:T(4,128)S(1)}, u32[]{:S(2)}, u32[]{:S(2)}) %collective-permute-start.25) | collective-permute-done | bytes 49184 | tf_op jit(solution)/shard_map/ppermute | solution.py:406
  129.4 3.5 %all-to-all-done.2.packed_ref = bf16[4,128,768]{2,1,0:T(8,128)(2,1)S(1)} async-done(((bf16[4,128,768]{2,1,0:T(8,128)(2,1)}), bf16[4,128,768]{2,1,0:T(8,128)(2,1)S(1)}, u32[]{:S(2)}, u32[]{:S(2)}) %all-to-all-start.2) | async-done | bytes 786464 | tf_op jit(solution)/shard_map/all_to_all | solution.py:412
  132.9 3.5 %all-to-all-start.3 = ((bf16[4,128,768]{2,1,0:T(8,128)(2,1)}), bf16[4,128,768]{2,1,0:T(8,128)(2,1)S(1)}, u32[]{:S(2)}, u32[]{:S(2)}) async-start(bf16[4,128,768]{2,1,0:T(8,128)(2,1)} %shard_map.167), calls=%async_computation.3 | async-start | bytes 1572864 | tf_op jit(solution)/shard_map/all_to_all | solution.py:412
  136.5 4.6 %collective-permute-start.27 = (f32[4,1,768]{2,1,0:T(1,128)S(1)}, f32[4,1,768]{2,1,0:T(1,128)S(1)}, u32[]{:S(2)}, u32[]{:S(2)}) collective-permute-start(f32[4,1,768]{2,1,0:T(1,128)S(1)} %slice.185), channel_id=1, source_target_pairs={{0,16},{4,20},{8,24},{12,28},{16,0},{20,4},{24,8},{28,12},{1,17},{... | collective-permute-start | bytes 36872 | tf_op jit(solution)/shard_map/ppermute | solution.py:406
  141.1 2.3 %shard_map.166 = (bf16[128,1536]{1,0:T(8,128)(2,1)}, bf16[128,1536]{1,0:T(8,128)(2,1)}) custom-call(bf16[4,128,768]{2,1,0:T(8,128)(2,1)} %copy-done.1), custom_call_target="tpu_custom_call" | custom-call | tf_op jit(solution)/shard_map/pallas_call | solution.py:106
  144.9 3.2 %all-to-all-done.3.packed_ref = bf16[4,128,768]{2,1,0:T(8,128)(2,1)S(1)} async-done(((bf16[4,128,768]{2,1,0:T(8,128)(2,1)}), bf16[4,128,768]{2,1,0:T(8,128)(2,1)S(1)}, u32[]{:S(2)}, u32[]{:S(2)}) %all-to-all-start.3) | async-done | bytes 786464 | tf_op jit(solution)/shard_map/all_to_all | solution.py:412
  148.9 2.3 %shard_map.168 = (bf16[128,1536]{1,0:T(8,128)(2,1)}, bf16[128,1536]{1,0:T(8,128)(2,1)}) custom-call(bf16[4,128,768]{2,1,0:T(8,128)(2,1)} %copy-done.2), custom_call_target="tpu_custom_call" | custom-call | tf_op jit(solution)/shard_map/pallas_call | solution.py:106
  (129 shorter events, 20.0 us)
Async XLA Ops:
  3.0 18.0 %all-to-all-start = ((bf16[4,144,768]{2,1,0:T(8,128)(2,1)}), bf16[4,144,768]{2,1,0:T(8,128)(2,1)S(1)}, u32[]{:S(2)}, u32[]{:S(2)}) async-start(bf16[4,144,768]{2,1,0:T(8,128)(2,1)} %shard_map.163), calls=%async_computation | async-start | bytes 1769472 | tf_op jit(solution)/shard_map/all_to_all | solution.py:412
  7.5 8.1 %collective-permute-start.3 = (bf16[4,1,768]{2,1,0:T(2,128)(2,1)S(1)}, bf16[4,1,768]{2,1,0:T(2,128)(2,1)S(1)}, u32[]{:S(2)}, u32[]{:S(2)}) collective-permute-start(bf16[4,1,768]{2,1,0:T(2,128)(2,1)S(1)} %copy.37), channel_id=1, source_target_pairs={{0,16},{4,20},{8,24},{12,28},{16,0},{20,4},{24,8},{28,12},{1,17},{... | collective-permute-start | bytes 18440 | tf_op jit(solution)/shard_map/ppermute | solution.py:406
  15.6 5.3 %collective-permute-start.4 = (bf16[4,2,768]{2,1,0:T(2,128)(2,1)S(1)}, bf16[4,2,768]{2,1,0:T(2,128)(2,1)S(1)}, u32[]{:S(2)}, u32[]{:S(2)}) collective-permute-start(bf16[4,2,768]{2,1,0:T(2,128)(2,1)S(1)} %pad_maximum_fusion.12), channel_id=1, source_target_pairs={{0,128},{32,160},{64,192},{96,224},{128,0},{160,32},{192,64},{224,... | collective-permute-start | bytes 36872 | tf_op jit(solution)/shard_map/ppermute | solution.py:406
  20.9 7.4 %collective-permute-start.5 = (bf16[4,4,768]{2,1,0:T(4,128)(2,1)S(1)}, bf16[4,4,768]{2,1,0:T(4,128)(2,1)S(1)}, u32[]{:S(2)}, u32[]{:S(2)}) collective-permute-start(bf16[4,4,768]{2,1,0:T(4,128)(2,1)S(1)} %pad_maximum_fusion.11), channel_id=1, source_target_pairs={{0,64},{32,96},{64,0},{96,32},{128,192},{160,224},{192,128},{224,1... | collective-permute-start | bytes 73736 | tf_op jit(solution)/shard_map/ppermute | solution.py:406
  21.6 9.7 %collective-permute-start = (bf16[64,768]{1,0:T(8,128)(2,1)S(1)}, bf16[64,768]{1,0:T(8,128)(2,1)S(1)}, u32[]{:S(2)}, u32[]{:S(2)}) collective-permute-start(bf16[64,768]{1,0:T(8,128)(2,1)S(1)} %bitcast.40), channel_id=1, source_target_pairs={{0,16},{4,20},{8,24},{12,28},{16,0},{20,4},{24,8},{28,12},{1,17},{... | collective-permute-start | bytes 294920 | tf_op jit(solution)/shard_map/ppermute | solution.py:406
  31.2 5.6 %collective-permute-start.6 = (bf16[2,8,768]{2,1,0:T(8,128)(2,1)S(1)}, bf16[2,8,768]{2,1,0:T(8,128)(2,1)S(1)}, u32[]{:S(2)}, u32[]{:S(2)}) collective-permute-start(bf16[2,8,768]{2,1,0:T(8,128)(2,1)S(1)} %get-tuple-element.89), channel_id=1, source_target_pairs={{0,8},{4,12},{8,0},{12,4},{16,24},{20,28},{24,16},{28,20},{1,9},{5... | collective-permute-start | bytes 73736 | tf_op jit(solution)/shard_map/ppermute | solution.py:406
  33.9 6.9 %collective-permute-start.2 = (bf16[144,768]{1,0:T(8,128)(2,1)S(1)}, bf16[144,768]{1,0:T(8,128)(2,1)S(1)}, u32[]{:S(2)}, u32[]{:S(2)}) collective-permute-start(bf16[144,768]{1,0:T(8,128)(2,1)S(1)} %pad_maximum_fusion.2), channel_id=1, source_target_pairs={{0,3},{1,0},{2,1},{3,2},{4,7},{5,4},{6,5},{7,6},{8,11},{9,8},{10,9... | collective-permute-start | bytes 663560 | tf_op jit(solution)/shard_map/ppermute | solution.py:388
  36.7 7.2 %collective-permute-start.1 = (bf16[144,768]{1,0:T(8,128)(2,1)S(1)}, bf16[144,768]{1,0:T(8,128)(2,1)S(1)}, u32[]{:S(2)}, u32[]{:S(2)}) collective-permute-start(bf16[144,768]{1,0:T(8,128)(2,1)S(1)} %pad_maximum_fusion.1), channel_id=1, source_target_pairs={{0,1},{1,2},{2,3},{3,0},{4,5},{5,6},{6,7},{7,4},{8,9},{9,10},{10,1... | collective-permute-start | bytes 663560 | tf_op jit(solution)/shard_map/ppermute | solution.py:388
  36.9 3.9 %collective-permute-start.7 = (bf16[1,16,768]{2,1,0:T(8,128)(2,1)S(1)}, bf16[1,16,768]{2,1,0:T(8,128)(2,1)S(1)}, u32[]{:S(2)}, u32[]{:S(2)}) collective-permute-start(bf16[1,16,768]{2,1,0:T(8,128)(2,1)S(1)} %get-tuple-element.87), channel_id=1, source_target_pairs={{0,4},{4,0},{8,12},{12,8},{16,20},{20,16},{24,28},{28,24},{1,5},{5... | collective-permute-start | bytes 73736 | tf_op jit(solution)/shard_map/ppermute | solution.py:406
  45.0 20.9 %collective-permute-start.9 = (bf16[864,768]{1,0:T(8,128)(2,1)S(1)}, bf16[864,768]{1,0:T(8,128)(2,1)}, u32[]{:S(2)}, u32[]{:S(2)}) collective-permute-start(bf16[864,768]{1,0:T(8,128)(2,1)S(1)} %pad_maximum_fusion.here_ref), channel_id=1, source_target_pairs={{0,240},{4,244},{8,248},{12,252},{16,224},{20,228},{24,232},{28,23... | collective-permute-start | bytes 3981320 | tf_op jit(solution)/shard_map/ppermute | solution.py:401
  45.0 20.9 %collective-permute-start.8 = (bf16[864,768]{1,0:T(8,128)(2,1)S(1)}, bf16[864,768]{1,0:T(8,128)(2,1)}, u32[]{:S(2)}, u32[]{:S(2)}) collective-permute-start(bf16[864,768]{1,0:T(8,128)(2,1)S(1)} %pad_maximum_fusion.here_ref), channel_id=1, source_target_pairs={{0,32},{4,36},{8,40},{12,44},{16,48},{20,52},{24,56},{28,60},{32,6... | collective-permute-start | bytes 3981320 | tf_op jit(solution)/shard_map/ppermute | solution.py:401
  47.0 15.9 %all-to-all-start.1 = ((bf16[4,128,768]{2,1,0:T(8,128)(2,1)}), bf16[4,128,768]{2,1,0:T(8,128)(2,1)S(1)}, u32[]{:S(2)}, u32[]{:S(2)}) async-start(bf16[4,128,768]{2,1,0:T(8,128)(2,1)} %shard_map.164), calls=%async_computation.1 | async-start | bytes 1572864 | tf_op jit(solution)/shard_map/all_to_all | solution.py:412
  50.5 5.7 %collective-permute-start.10 = (bf16[1,32,768]{2,1,0:T(8,128)(2,1)S(1)}, bf16[1,32,768]{2,1,0:T(8,128)(2,1)S(1)}, u32[]{:S(2)}, u32[]{:S(2)}) collective-permute-start(bf16[1,32,768]{2,1,0:T(8,128)(2,1)S(1)} %pad_maximum_fusion.9), channel_id=1, source_target_pairs={{0,2},{1,3},{2,0},{3,1},{4,6},{5,7},{6,4},{7,5},{8,10},{9,11},{10,... | collective-permute-start | bytes 147464 | tf_op jit(solution)/shard_map/ppermute | solution.py:406
  56.2 5.7 %collective-permute-start.11 = (bf16[1,64,768]{2,1,0:T(8,128)(2,1)S(1)}, bf16[1,64,768]{2,1,0:T(8,128)(2,1)S(1)}, u32[]{:S(2)}, u32[]{:S(2)}) collective-permute-start(bf16[1,64,768]{2,1,0:T(8,128)(2,1)S(1)} %pad_maximum_fusion.4), channel_id=1, source_target_pairs={{0,1},{1,0},{2,3},{3,2},{4,5},{5,4},{6,7},{7,6},{8,9},{9,8},{10,11... | collective-permute-start | bytes 294920 | tf_op jit(solution)/shard_map/ppermute | solution.py:406
  62.9 2.1 %collective-permute-start.12 = (bf16[1,128,768]{2,1,0:T(8,128)(2,1)S(1)}, bf16[1,128,768]{2,1,0:T(8,128)(2,1)S(1)}, u32[]{:S(2)}, u32[]{:S(2)}) collective-permute-start(bf16[1,128,768]{2,1,0:T(8,128)(2,1)S(1)} %pad_maximum_fusion.3), channel_id=1, source_target_pairs={{0,32},{32,0},{64,96},{96,64},{128,160},{160,128},{192,224},{224,1... | collective-permute-start | bytes 589832 | tf_op jit(solution)/shard_map/ppermute | solution.py:406
  79.8 2.6 %collective-permute-start.20 = (f32[1,128,768]{2,1,0:T(8,128)}, f32[1,128,768]{2,1,0:T(8,128)S(1)}, u32[]{:S(2)}, u32[]{:S(2)}) collective-permute-start(f32[1,128,768]{2,1,0:T(8,128)} %bitcast.46), channel_id=1, source_target_pairs={{0,32},{32,0},{64,96},{96,64},{128,160},{160,128},{192,224},{224,1... | collective-permute-start | bytes 1179656 | tf_op jit(solution)/shard_map/ppermute | solution.py:406
  80.5 9.1 %collective-permute-start.13 = (bf16[352,768]{1,0:T(8,128)(2,1)}, bf16[352,768]{1,0:T(8,128)(2,1)S(1)}, u32[]{:S(2)}, u32[]{:S(2)}) collective-permute-start(bf16[352,768]{1,0:T(8,128)(2,1)} %get-tuple-element.47), channel_id=1, source_target_pairs={{0,240},{4,244},{8,248},{12,252},{16,224},{20,228},{24,232},{28,23... | collective-permute-start | bytes 1622024 | tf_op jit(solution)/shard_map/ppermute | solution.py:401
  82.4 9.0 %collective-permute-start.14 = (bf16[352,768]{1,0:T(8,128)(2,1)}, bf16[352,768]{1,0:T(8,128)(2,1)S(1)}, u32[]{:S(2)}, u32[]{:S(2)}) collective-permute-start(bf16[352,768]{1,0:T(8,128)(2,1)} %get-tuple-element.48), channel_id=1, source_target_pairs={{0,32},{4,36},{8,40},{12,44},{16,48},{20,52},{24,56},{28,60},{32,6... | collective-permute-start | bytes 1622024 | tf_op jit(solution)/shard_map/ppermute | solution.py:401
  83.5 13.2 %collective-permute-start.21 = (f32[1,64,768]{2,1,0:T(8,128)S(1)}, f32[1,64,768]{2,1,0:T(8,128)S(1)}, u32[]{:S(2)}, u32[]{:S(2)}) collective-permute-start(f32[1,64,768]{2,1,0:T(8,128)S(1)} %get-tuple-element.72), channel_id=1, source_target_pairs={{0,1},{1,0},{2,3},{3,2},{4,5},{5,4},{6,7},{7,6},{8,9},{9,8},{10,11... | collective-permute-start | bytes 589832 | tf_op jit(solution)/shard_map/ppermute | solution.py:406
  91.4 23.9 %collective-permute-start.15 = (bf16[512,768]{1,0:T(8,128)(2,1)S(1)}, bf16[512,768]{1,0:T(8,128)(2,1)S(1)}, u32[]{:S(2)}, u32[]{:S(2)}) collective-permute-start(bf16[512,768]{1,0:T(8,128)(2,1)S(1)} %copy-done.16), channel_id=1, source_target_pairs={{0,240},{4,244},{8,248},{12,252},{16,224},{20,228},{24,232},{28,23... | collective-permute-start | bytes 2359304 | tf_op jit(solution)/shard_map/ppermute | solution.py:401
  91.7 23.6 %collective-permute-start.16 = (bf16[512,768]{1,0:T(8,128)(2,1)S(1)}, bf16[512,768]{1,0:T(8,128)(2,1)S(1)}, u32[]{:S(2)}, u32[]{:S(2)}) collective-permute-start(bf16[512,768]{1,0:T(8,128)(2,1)S(1)} %copy-done.15), channel_id=1, source_target_pairs={{0,32},{4,36},{8,40},{12,44},{16,48},{20,52},{24,56},{28,60},{32,6... | collective-permute-start | bytes 2359304 | tf_op jit(solution)/shard_map/ppermute | solution.py:401
  93.4 11.2 %collective-permute-start.17 = (bf16[144,768]{1,0:T(8,128)(2,1)S(1)}, bf16[144,768]{1,0:T(8,128)(2,1)S(1)}, u32[]{:S(2)}, u32[]{:S(2)}) collective-permute-start(bf16[144,768]{1,0:T(8,128)(2,1)S(1)} %get-tuple-element.70), channel_id=1, source_target_pairs={{0,1},{1,2},{2,3},{3,0},{4,5},{5,6},{6,7},{7,4},{8,9},{9,10},{10,1... | collective-permute-start | bytes 663560 | tf_op jit(solution)/shard_map/ppermute | solution.py:388
  93.5 11.2 %collective-permute-start.18 = (bf16[144,768]{1,0:T(8,128)(2,1)S(1)}, bf16[144,768]{1,0:T(8,128)(2,1)S(1)}, u32[]{:S(2)}, u32[]{:S(2)}) collective-permute-start(bf16[144,768]{1,0:T(8,128)(2,1)S(1)} %get-tuple-element.71), channel_id=1, source_target_pairs={{0,3},{1,0},{2,1},{3,2},{4,7},{5,4},{6,5},{7,6},{8,11},{9,8},{10,9... | collective-permute-start | bytes 663560 | tf_op jit(solution)/shard_map/ppermute | solution.py:388
  96.7 13.8 %collective-permute-start.22 = (f32[1,32,768]{2,1,0:T(8,128)S(1)}, f32[1,32,768]{2,1,0:T(8,128)S(1)}, u32[]{:S(2)}, u32[]{:S(2)}) collective-permute-start(f32[1,32,768]{2,1,0:T(8,128)S(1)} %get-tuple-element.74), channel_id=1, source_target_pairs={{0,2},{1,3},{2,0},{3,1},{4,6},{5,7},{6,4},{7,5},{8,10},{9,11},{10,... | collective-permute-start | bytes 294920 | tf_op jit(solution)/shard_map/ppermute | solution.py:406
  104.7 10.6 %collective-permute-start.19 = (bf16[64,768]{1,0:T(8,128)(2,1)S(1)}, bf16[64,768]{1,0:T(8,128)(2,1)S(1)}, u32[]{:S(2)}, u32[]{:S(2)}) collective-permute-start(bf16[64,768]{1,0:T(8,128)(2,1)S(1)} %pad_maximum_fusion.5), channel_id=1, source_target_pairs={{0,16},{4,20},{8,24},{12,28},{16,0},{20,4},{24,8},{28,12},{1,17},{... | collective-permute-start | bytes 294920 | tf_op jit(solution)/shard_map/ppermute | solution.py:406
  110.5 4.2 %collective-permute-start.23 = (f32[1,16,768]{2,1,0:T(8,128)S(1)}, f32[1,16,768]{2,1,0:T(8,128)S(1)}, u32[]{:S(2)}, u32[]{:S(2)}) collective-permute-start(f32[1,16,768]{2,1,0:T(8,128)S(1)} %get-tuple-element.82), channel_id=1, source_target_pairs={{0,4},{4,0},{8,12},{12,8},{16,20},{20,16},{24,28},{28,24},{1,5},{5... | collective-permute-start | bytes 147464 | tf_op jit(solution)/shard_map/ppermute | solution.py:406
  115.3 8.2 %collective-permute-start.24 = (f32[2,8,768]{2,1,0:T(8,128)S(1)}, f32[2,8,768]{2,1,0:T(8,128)S(1)}, u32[]{:S(2)}, u32[]{:S(2)}) collective-permute-start(f32[2,8,768]{2,1,0:T(8,128)S(1)} %get-tuple-element.78), channel_id=1, source_target_pairs={{0,8},{4,12},{8,0},{12,4},{16,24},{20,28},{24,16},{28,20},{1,9},{5... | collective-permute-start | bytes 147464 | tf_op jit(solution)/shard_map/ppermute | solution.py:406
  117.0 16.0 %all-to-all-start.2 = ((bf16[4,128,768]{2,1,0:T(8,128)(2,1)}), bf16[4,128,768]{2,1,0:T(8,128)(2,1)S(1)}, u32[]{:S(2)}, u32[]{:S(2)}) async-start(bf16[4,128,768]{2,1,0:T(8,128)(2,1)} %get-tuple-element.42), calls=%async_computation.2 | async-start | bytes 1572864 | tf_op jit(solution)/shard_map/all_to_all | solution.py:412
  123.5 5.8 %collective-permute-start.25 = (f32[4,4,768]{2,1,0:T(4,128)S(1)}, f32[4,4,768]{2,1,0:T(4,128)S(1)}, u32[]{:S(2)}, u32[]{:S(2)}) collective-permute-start(f32[4,4,768]{2,1,0:T(4,128)S(1)} %pad_maximum_fusion.6), channel_id=1, source_target_pairs={{0,64},{32,96},{64,0},{96,32},{128,192},{160,224},{192,128},{224,1... | collective-permute-start | bytes 147464 | tf_op jit(solution)/shard_map/ppermute | solution.py:406
  129.3 7.2 %collective-permute-start.26 = (f32[4,2,768]{2,1,0:T(2,128)S(1)}, f32[4,2,768]{2,1,0:T(2,128)S(1)}, u32[]{:S(2)}, u32[]{:S(2)}) collective-permute-start(f32[4,2,768]{2,1,0:T(2,128)S(1)} %slice.183), channel_id=1, source_target_pairs={{0,128},{32,160},{64,192},{96,224},{128,0},{160,32},{192,64},{224,... | collective-permute-start | bytes 73736 | tf_op jit(solution)/shard_map/ppermute | solution.py:406
  132.9 15.1 %all-to-all-start.3 = ((bf16[4,128,768]{2,1,0:T(8,128)(2,1)}), bf16[4,128,768]{2,1,0:T(8,128)(2,1)S(1)}, u32[]{:S(2)}, u32[]{:S(2)}) async-start(bf16[4,128,768]{2,1,0:T(8,128)(2,1)} %shard_map.167), calls=%async_computation.3 | async-start | bytes 1572864 | tf_op jit(solution)/shard_map/all_to_all | solution.py:412
  136.5 7.7 %collective-permute-start.27 = (f32[4,1,768]{2,1,0:T(1,128)S(1)}, f32[4,1,768]{2,1,0:T(1,128)S(1)}, u32[]{:S(2)}, u32[]{:S(2)}) collective-permute-start(f32[4,1,768]{2,1,0:T(1,128)S(1)} %slice.185), channel_id=1, source_target_pairs={{0,16},{4,20},{8,24},{12,28},{16,0},{20,4},{24,8},{28,12},{1,17},{... | collective-permute-start | bytes 36872 | tf_op jit(solution)/shard_map/ppermute | solution.py:406
  (18 other events, 154.5 us)

commit v3 on v2

--- a/solution.py
+++ b/solution.py
@@ -529,6 +529,7 @@
     back = steps[::-1]
     text_grad = sent_text(text_grad[None], text_away[None], *back[0])
     text_grad = scatter_text(text_grad, *back[1])
+    text_grad = scatter_text(text_grad, *back[2])
     od_in = regrouped(od)
     halo = here_grad[OWN:] + halo_first.astype(F32) + halo_second.astype(F32)
     side = SIDE + TILE
@@ -537,7 +538,7 @@
     rim_grad = halo[2 * side :]
     right = turned_width(to_left, -1)
     left = turned_width(to_right, 1)
-    text_grad = scatter_text(text_grad, *back[2], to_left, to_right)
+    text_grad = scatter_text(text_grad, *back[3], to_left, to_right, od_in)
     rim_out = jnp.concatenate(
         [
             rim_grad[:TILE] + left[SIDE:].astype(F32),
@@ -547,11 +548,11 @@
         0,
     ).astype(BF16)
     rim_in = swapped(rim_out, "ha", GROUP)
-    text_grad = scatter_text(text_grad, *back[3], rim_out)
-    text_grad = scatter_text(text_grad, *back[4], rim_in, first, second)
+    text_grad = scatter_text(text_grad, *back[4], rim_out)
+    text_grad = scatter_text(text_grad, *back[5], rim_in, first, second)
     grads = settle(half.reshape(1), here_grad, first, second, rim_in, left, right)
-    text_grad = scatter_text(text_grad, *back[5], grads)
-    for step in back[6:]:
+    text_grad = scatter_text(text_grad, *back[6], grads)
+    for step in back[7:]:
         text_grad = scatter_text(text_grad, *step)
     text_grad = joined_text(text_grad)
     attended, query_grad = unpack(od_in)

time: 152 us -> 145 us (0.954)
  waiting for transfers between devices: 52 us -> 39.8 us
  local copies, waits for them, and re-layouts: 2.97 us -> 5.39 us
    ppermute x4, waiting for transfers between devices: 10.9 us -> 5.9 us  [turned_width(): lax.ppermute(value, 'wa', [(i, (i + step) % count) for i in range(count)])]
    all_to_all x4, waiting for transfers between devices: 7.72 us -> 3.91 us  [regrouped(): return lax.all_to_all(value, 'ha', 0, 0, axis_index_groups=groups)]
    ppermute x6, waiting for transfers between devices: 7.81 us -> 5.3 us  [turned_time(): return lax.ppermute(value, ('ta', 'ha'), pairs)]
  transfers between devices with their start and end apart: 32 -> 32, of which waited for: 17 -> 18; matrix products, arithmetic and copies ran while one was open for 4% -> 7% of each run, Pallas kernels for 5% -> 5%
where the time goes in v3:
time: 145 us; the launch traced here: 144 us
  starting transfers between devices  63.7 us (44%)
  waiting for transfers between devices  39.8 us (27%)
  Pallas kernels  26 us (18%)
  other arithmetic  7.05 us (5%)
  local copies, waits for them, and re-layouts  5.39 us (4%)
  between operations  1.71 us (1%)
    ppermute x18, starting transfers between devices, swapped(): return lax.ppermute(value, axis, [(i, i ^ bit) for i in range(count)])  38.7 us
    ppermute x18, waiting for transfers between devices, swapped(): return lax.ppermute(value, axis, [(i, i ^ bit) for i in range(count)])  24.7 us
    all_to_all x4, starting transfers between devices, regrouped(): return lax.all_to_all(value, 'ha', 0, 0, axis_index_groups=groups)  15.9 us
    pallas_call x1, Pallas kernels, attention(): pl.pallas_call(functools.partial(attention_kernel, text_bits), grid=(head...  14 us
    ppermute x4, starting transfers between devices, turned_width(): lax.ppermute(value, 'wa', [(i, (i + step) % count) for i in range(count)])  6.15 us
    ppermute x4, waiting for transfers between devices, turned_width(): lax.ppermute(value, 'wa', [(i, (i + step) % count) for i in range(count)])  5.9 us
    ppermute x6, waiting for transfers between devices, turned_time(): return lax.ppermute(value, ('ta', 'ha'), pairs)  5.3 us
    pallas_call x2, Pallas kernels, pack(): pl.pallas_call(pack_kernel, grid=(PACKS,), in_specs=specs, out_specs=pl.B...  4.62 us
  transfers between devices with their start and end apart: 32, of which 18 were waited for; matrix products, arithmetic and copies ran while one was open for 7% of the time, Pallas kernels for 5%

profile of v3, /device:TPU:32, one launch (start us, length us, event | category | flops | bytes accessed | tf_op | source)
XLA Modules:
  0.0 143.7 jit_solution(17343765258367684987)
XLA Ops:
  0.7 2.3 %shard_map.163 = bf16[4,144,768]{2,1,0:T(8,128)(2,1)} custom-call(bf16[128,1536]{1,0:T(8,128)(2,1)} %bitcast.36, bf16[128,1536]{1,0:T(8,128)(2,1)} %bitcast.37, s32[8,27]{1,0:T(8,128)} %bitcast.43), custom_call_target="tpu_custom_call" | custom-call | tf_op jit(solution)/shard_map/pallas_call | solution.py:78
  3.0 4.5 %all-to-all-start = ((bf16[4,144,768]{2,1,0:T(8,128)(2,1)}), bf16[4,144,768]{2,1,0:T(8,128)(2,1)S(1)}, u32[]{:S(2)}, u32[]{:S(2)}) async-start(bf16[4,144,768]{2,1,0:T(8,128)(2,1)} %shard_map.163), calls=%async_computation | async-start | bytes 1769472 | tf_op jit(solution)/shard_map/all_to_all | solution.py:412
  7.5 6.4 %collective-permute-start.3 = (bf16[4,1,768]{2,1,0:T(2,128)(2,1)S(1)}, bf16[4,1,768]{2,1,0:T(2,128)(2,1)S(1)}, u32[]{:S(2)}, u32[]{:S(2)}) collective-permute-start(bf16[4,1,768]{2,1,0:T(2,128)(2,1)S(1)} %copy.37), channel_id=1, source_target_pairs={{0,16},{4,20},{8,24},{12,28},{16,0},{20,4},{24,8},{28,12},{1,17},{... | collective-permute-start | bytes 18440 | tf_op jit(solution)/shard_map/ppermute | solution.py:406
  13.9 1.7 %collective-permute-done.3 = bf16[4,1,768]{2,1,0:T(2,128)(2,1)S(1)} collective-permute-done((bf16[4,1,768]{2,1,0:T(2,128)(2,1)S(1)}, bf16[4,1,768]{2,1,0:T(2,128)(2,1)S(1)}, u32[]{:S(2)}, u32[]{:S(2)}) %collective-permute-start.3) | collective-permute-done | bytes 6176 | tf_op jit(solution)/shard_map/ppermute | solution.py:406
  15.6 3.0 %collective-permute-start.4 = (bf16[4,2,768]{2,1,0:T(2,128)(2,1)S(1)}, bf16[4,2,768]{2,1,0:T(2,128)(2,1)S(1)}, u32[]{:S(2)}, u32[]{:S(2)}) collective-permute-start(bf16[4,2,768]{2,1,0:T(2,128)(2,1)S(1)} %pad_maximum_fusion.12), channel_id=1, source_target_pairs={{0,128},{32,160},{64,192},{96,224},{128,0},{160,32},{192,64},{224,... | collective-permute-start | bytes 36872 | tf_op jit(solution)/shard_map/ppermute | solution.py:406
  18.6 2.3 %shard_map.164 = bf16[4,128,768]{2,1,0:T(8,128)(2,1)} custom-call(bf16[128,1536]{1,0:T(8,128)(2,1)} %bitcast.38, bf16[128,1536]{1,0:T(8,128)(2,1)} %bitcast.39), custom_call_target="tpu_custom_call" | custom-call | tf_op jit(solution)/shard_map/pallas_call | solution.py:78
  21.6 6.7 %collective-permute-start = (bf16[64,768]{1,0:T(8,128)(2,1)S(1)}, bf16[64,768]{1,0:T(8,128)(2,1)S(1)}, u32[]{:S(2)}, u32[]{:S(2)}) collective-permute-start(bf16[64,768]{1,0:T(8,128)(2,1)S(1)} %bitcast.40), channel_id=1, source_target_pairs={{0,16},{4,20},{8,24},{12,28},{16,0},{20,4},{24,8},{28,12},{1,17},{... | collective-permute-start | bytes 294920 | tf_op jit(solution)/shard_map/ppermute | solution.py:406
  28.3 2.9 %collective-permute-done = bf16[64,768]{1,0:T(8,128)(2,1)S(1)} collective-permute-done((bf16[64,768]{1,0:T(8,128)(2,1)S(1)}, bf16[64,768]{1,0:T(8,128)(2,1)S(1)}, u32[]{:S(2)}, u32[]{:S(2)}) %collective-permute-start) | collective-permute-done | bytes 98336 | tf_op jit(solution)/shard_map/ppermute | solution.py:406
  31.3 2.6 %collective-permute-start.6 = (bf16[2,8,768]{2,1,0:T(8,128)(2,1)S(1)}, bf16[2,8,768]{2,1,0:T(8,128)(2,1)S(1)}, u32[]{:S(2)}, u32[]{:S(2)}) collective-permute-start(bf16[2,8,768]{2,1,0:T(8,128)(2,1)S(1)} %get-tuple-element.89), channel_id=1, source_target_pairs={{0,8},{4,12},{8,0},{12,4},{16,24},{20,28},{24,16},{28,20},{1,9},{5... | collective-permute-start | bytes 73736 | tf_op jit(solution)/shard_map/ppermute | solution.py:406
  33.9 2.8 %collective-permute-start.2 = (bf16[144,768]{1,0:T(8,128)(2,1)S(1)}, bf16[144,768]{1,0:T(8,128)(2,1)S(1)}, u32[]{:S(2)}, u32[]{:S(2)}) collective-permute-start(bf16[144,768]{1,0:T(8,128)(2,1)S(1)} %pad_maximum_fusion.2), channel_id=1, source_target_pairs={{0,3},{1,0},{2,1},{3,2},{4,7},{5,4},{6,5},{7,6},{8,11},{9,8},{10,9... | collective-permute-start | bytes 663560 | tf_op jit(solution)/shard_map/ppermute | solution.py:388
  37.8 3.0 %collective-permute-done.7 = bf16[1,16,768]{2,1,0:T(8,128)(2,1)S(1)} collective-permute-done((bf16[1,16,768]{2,1,0:T(8,128)(2,1)S(1)}, bf16[1,16,768]{2,1,0:T(8,128)(2,1)S(1)}, u32[]{:S(2)}, u32[]{:S(2)}) %collective-permute-start.7) | collective-permute-done | bytes 24608 | tf_op jit(solution)/shard_map/ppermute | solution.py:406
  40.8 3.2 %collective-permute-done.1 = bf16[144,768]{1,0:T(8,128)(2,1)S(1)} collective-permute-done((bf16[144,768]{1,0:T(8,128)(2,1)S(1)}, bf16[144,768]{1,0:T(8,128)(2,1)S(1)}, u32[]{:S(2)}, u32[]{:S(2)}) %collective-permute-start.1) | collective-permute-done | bytes 221216 | tf_op jit(solution)/shard_map/ppermute | solution.py:388
  47.0 3.5 %all-to-all-start.1 = ((bf16[4,128,768]{2,1,0:T(8,128)(2,1)}), bf16[4,128,768]{2,1,0:T(8,128)(2,1)S(1)}, u32[]{:S(2)}, u32[]{:S(2)}) async-start(bf16[4,128,768]{2,1,0:T(8,128)(2,1)} %shard_map.164), calls=%async_computation.1 | async-start | bytes 1572864 | tf_op jit(solution)/shard_map/all_to_all | solution.py:412
  50.6 5.6 %collective-permute-done.10 = bf16[1,32,768]{2,1,0:T(8,128)(2,1)S(1)} collective-permute-done((bf16[1,32,768]{2,1,0:T(8,128)(2,1)S(1)}, bf16[1,32,768]{2,1,0:T(8,128)(2,1)S(1)}, u32[]{:S(2)}, u32[]{:S(2)}) %collective-permute-start.10) | collective-permute-done | bytes 49184 | tf_op jit(solution)/shard_map/ppermute | solution.py:406
  56.8 5.1 %collective-permute-done.11 = bf16[1,64,768]{2,1,0:T(8,128)(2,1)S(1)} collective-permute-done((bf16[1,64,768]{2,1,0:T(8,128)(2,1)S(1)}, bf16[1,64,768]{2,1,0:T(8,128)(2,1)S(1)}, u32[]{:S(2)}, u32[]{:S(2)}) %collective-permute-start.11) | collective-permute-done | bytes 98336 | tf_op jit(solution)/shard_map/ppermute | solution.py:406
  65.9 14.0 %shard_map.165 = (bf16[4,128,768]{2,1,0:T(8,128)(2,1)}, f32[864,768]{1,0:T(8,128)}, bf16[512,768]{1,0:T(8,128)(2,1)}, bf16[512,768]{1,0:T(8,128)(2,1)}, bf16[352...) custom-call(s32[2]{0:T(128)} %pad_add_fusion.length_ref, ...), custom_call_target="tpu_custom_call" | custom-call | tf_op jit(solution)/shard_map/pallas_call | solution.py:282
  80.5 1.9 %collective-permute-start.13 = (bf16[352,768]{1,0:T(8,128)(2,1)}, bf16[352,768]{1,0:T(8,128)(2,1)S(1)}, u32[]{:S(2)}, u32[]{:S(2)}) collective-permute-start(bf16[352,768]{1,0:T(8,128)(2,1)} %get-tuple-element.47), channel_id=1, source_target_pairs={{0,240},{4,244},{8,248},{12,252},{16,224},{20,228},{24,232},{28,23... | collective-permute-start | bytes 1622024 | tf_op jit(solution)/shard_map/ppermute | solution.py:401
  82.4 3.5 %all-to-all-start.2 = ((bf16[4,128,768]{2,1,0:T(8,128)(2,1)}), bf16[4,128,768]{2,1,0:T(8,128)(2,1)S(1)}, u32[]{:S(2)}, u32[]{:S(2)}) async-start(bf16[4,128,768]{2,1,0:T(8,128)(2,1)} %get-tuple-element.42), calls=%async_computation.2 | async-start | bytes 1572864 | tf_op jit(solution)/shard_map/all_to_all | solution.py:412
  86.1 3.5 %collective-permute-done.13 = bf16[352,768]{1,0:T(8,128)(2,1)S(1)} collective-permute-done((bf16[352,768]{1,0:T(8,128)(2,1)}, bf16[352,768]{1,0:T(8,128)(2,1)S(1)}, u32[]{:S(2)}, u32[]{:S(2)}) %collective-permute-start.13) | collective-permute-done | bytes 540704 | tf_op jit(solution)/shard_map/ppermute | solution.py:401
  89.6 1.8 %collective-permute-done.14 = bf16[352,768]{1,0:T(8,128)(2,1)S(1)} collective-permute-done((bf16[352,768]{1,0:T(8,128)(2,1)}, bf16[352,768]{1,0:T(8,128)(2,1)S(1)}, u32[]{:S(2)}, u32[]{:S(2)}) %collective-permute-start.14) | collective-permute-done | bytes 540704 | tf_op jit(solution)/shard_map/ppermute | solution.py:401
  97.1 2.4 %collective-permute-start.18 = (bf16[144,768]{1,0:T(8,128)(2,1)}, bf16[144,768]{1,0:T(8,128)(2,1)}, u32[]{:S(2)}, u32[]{:S(2)}) collective-permute-start(bf16[144,768]{1,0:T(8,128)(2,1)} %get-tuple-element.71), channel_id=1, source_target_pairs={{0,3},{1,0},{2,1},{3,2},{4,7},{5,4},{6,5},{7,6},{8,11},{9,8},{10,9... | collective-permute-start | bytes 663560 | tf_op jit(solution)/shard_map/ppermute | solution.py:388
  101.7 1.8 %collective-permute-start.23 = (f32[1,16,768]{2,1,0:T(8,128)S(1)}, f32[1,16,768]{2,1,0:T(8,128)S(1)}, u32[]{:S(2)}, u32[]{:S(2)}) collective-permute-start(f32[1,16,768]{2,1,0:T(8,128)S(1)} %get-tuple-element.82), channel_id=1, source_target_pairs={{0,4},{4,0},{8,12},{12,8},{16,20},{20,16},{24,28},{28,24},{1,5},{5... | collective-permute-start | bytes 147464 | tf_op jit(solution)/shard_map/ppermute | solution.py:406
  103.4 2.5 %collective-permute-done.17.left_ref = bf16[144,768]{1,0:T(8,128)(2,1)} collective-permute-done((bf16[144,768]{1,0:T(8,128)(2,1)}, bf16[144,768]{1,0:T(8,128)(2,1)}, u32[]{:S(2)}, u32[]{:S(2)}) %collective-permute-start.17) | collective-permute-done | bytes 221216 | tf_op jit(solution)/shard_map/ppermute | solution.py:388
  107.7 5.7 %collective-permute-start.19 = (bf16[64,768]{1,0:T(8,128)(2,1)S(1)}, bf16[64,768]{1,0:T(8,128)(2,1)S(1)}, u32[]{:S(2)}, u32[]{:S(2)}) collective-permute-start(bf16[64,768]{1,0:T(8,128)(2,1)S(1)} %pad_maximum_fusion.5), channel_id=1, source_target_pairs={{0,16},{4,20},{8,24},{12,28},{16,0},{20,4},{24,8},{28,12},{1,17},{... | collective-permute-start | bytes 294920 | tf_op jit(solution)/shard_map/ppermute | solution.py:406
  113.4 3.0 %collective-permute-start.24 = (f32[2,8,768]{2,1,0:T(8,128)S(1)}, f32[2,8,768]{2,1,0:T(8,128)S(1)}, u32[]{:S(2)}, u32[]{:S(2)}) collective-permute-start(f32[2,8,768]{2,1,0:T(8,128)S(1)} %get-tuple-element.78), channel_id=1, source_target_pairs={{0,8},{4,12},{8,0},{12,4},{16,24},{20,28},{24,16},{28,20},{1,9},{5... | collective-permute-start | bytes 147464 | tf_op jit(solution)/shard_map/ppermute | solution.py:406
  116.4 2.7 %collective-permute-done.24 = f32[2,8,768]{2,1,0:T(8,128)S(1)} collective-permute-done((f32[2,8,768]{2,1,0:T(8,128)S(1)}, f32[2,8,768]{2,1,0:T(8,128)S(1)}, u32[]{:S(2)}, u32[]{:S(2)}) %collective-permute-start.24) | collective-permute-done | bytes 49184 | tf_op jit(solution)/shard_map/ppermute | solution.py:406
  120.3 2.9 %shard_map.167 = bf16[4,128,768]{2,1,0:T(8,128)(2,1)} custom-call(s32[1]{0:T(128)} %bitcast.18.half_ref, f32[864,768]{1,0:T(8,128)} %get-tuple-element.45.own_ref, bf16[512,768]{1,0:T(8,128)(2,1)} %copy-done.4, bf16[512,768]{1,0:T(8,128)(2,1)} %copy-done.5, bf16[64,768]{1,0:T(8,128)(2,1)} %copy-done.9, bf16[144,768]{1,0:T(8,128)(2,1)} %collective-permute-done.17.left_ref, ...), custom_call_target="tpu_custom_call" | custom-call | tf_op jit(solution)/shard_map/pallas_call | solution.py:340
  124.8 4.4 %all-to-all-start.3 = ((bf16[4,128,768]{2,1,0:T(8,128)(2,1)}), bf16[4,128,768]{2,1,0:T(8,128)(2,1)S(1)}, u32[]{:S(2)}, u32[]{:S(2)}) async-start(bf16[4,128,768]{2,1,0:T(8,128)(2,1)} %shard_map.167), calls=%async_computation.3 | async-start | bytes 1572864 | tf_op jit(solution)/shard_map/all_to_all | solution.py:412
  129.3 4.2 %collective-permute-start.27 = (f32[4,1,768]{2,1,0:T(1,128)S(1)}, f32[4,1,768]{2,1,0:T(1,128)S(1)}, u32[]{:S(2)}, u32[]{:S(2)}) collective-permute-start(f32[4,1,768]{2,1,0:T(1,128)S(1)} %slice.185), channel_id=1, source_target_pairs={{0,16},{4,20},{8,24},{12,28},{16,0},{20,4},{24,8},{28,12},{1,17},{... | collective-permute-start | bytes 36872 | tf_op jit(solution)/shard_map/ppermute | solution.py:406
  133.5 2.3 %shard_map.166 = (bf16[128,1536]{1,0:T(8,128)(2,1)}, bf16[128,1536]{1,0:T(8,128)(2,1)}) custom-call(bf16[4,128,768]{2,1,0:T(8,128)(2,1)} %copy-done.1), custom_call_target="tpu_custom_call" | custom-call | tf_op jit(solution)/shard_map/pallas_call | solution.py:106
  137.7 2.9 %all-to-all-done.3.packed_ref = bf16[4,128,768]{2,1,0:T(8,128)(2,1)S(1)} async-done(((bf16[4,128,768]{2,1,0:T(8,128)(2,1)}), bf16[4,128,768]{2,1,0:T(8,128)(2,1)S(1)}, u32[]{:S(2)}, u32[]{:S(2)}) %all-to-all-start.3) | async-done | bytes 786464 | tf_op jit(solution)/shard_map/all_to_all | solution.py:412
  141.5 2.3 %shard_map.168 = (bf16[128,1536]{1,0:T(8,128)(2,1)}, bf16[128,1536]{1,0:T(8,128)(2,1)}) custom-call(bf16[4,128,768]{2,1,0:T(8,128)(2,1)} %copy-done.2), custom_call_target="tpu_custom_call" | custom-call | tf_op jit(solution)/shard_map/pallas_call | solution.py:106
  (123 shorter events, 24.9 us)
Async XLA Ops:
  3.0 18.0 %all-to-all-start = ((bf16[4,144,768]{2,1,0:T(8,128)(2,1)}), bf16[4,144,768]{2,1,0:T(8,128)(2,1)S(1)}, u32[]{:S(2)}, u32[]{:S(2)}) async-start(bf16[4,144,768]{2,1,0:T(8,128)(2,1)} %shard_map.163), calls=%async_computation | async-start | bytes 1769472 | tf_op jit(solution)/shard_map/all_to_all | solution.py:412
  7.5 8.1 %collective-permute-start.3 = (bf16[4,1,768]{2,1,0:T(2,128)(2,1)S(1)}, bf16[4,1,768]{2,1,0:T(2,128)(2,1)S(1)}, u32[]{:S(2)}, u32[]{:S(2)}) collective-permute-start(bf16[4,1,768]{2,1,0:T(2,128)(2,1)S(1)} %copy.37), channel_id=1, source_target_pairs={{0,16},{4,20},{8,24},{12,28},{16,0},{20,4},{24,8},{28,12},{1,17},{... | collective-permute-start | bytes 18440 | tf_op jit(solution)/shard_map/ppermute | solution.py:406
  15.6 5.3 %collective-permute-start.4 = (bf16[4,2,768]{2,1,0:T(2,128)(2,1)S(1)}, bf16[4,2,768]{2,1,0:T(2,128)(2,1)S(1)}, u32[]{:S(2)}, u32[]{:S(2)}) collective-permute-start(bf16[4,2,768]{2,1,0:T(2,128)(2,1)S(1)} %pad_maximum_fusion.12), channel_id=1, source_target_pairs={{0,128},{32,160},{64,192},{96,224},{128,0},{160,32},{192,64},{224,... | collective-permute-start | bytes 36872 | tf_op jit(solution)/shard_map/ppermute | solution.py:406
  20.9 7.4 %collective-permute-start.5 = (bf16[4,4,768]{2,1,0:T(4,128)(2,1)S(1)}, bf16[4,4,768]{2,1,0:T(4,128)(2,1)S(1)}, u32[]{:S(2)}, u32[]{:S(2)}) collective-permute-start(bf16[4,4,768]{2,1,0:T(4,128)(2,1)S(1)} %pad_maximum_fusion.11), channel_id=1, source_target_pairs={{0,64},{32,96},{64,0},{96,32},{128,192},{160,224},{192,128},{224,1... | collective-permute-start | bytes 73736 | tf_op jit(solution)/shard_map/ppermute | solution.py:406
  21.6 9.7 %collective-permute-start = (bf16[64,768]{1,0:T(8,128)(2,1)S(1)}, bf16[64,768]{1,0:T(8,128)(2,1)S(1)}, u32[]{:S(2)}, u32[]{:S(2)}) collective-permute-start(bf16[64,768]{1,0:T(8,128)(2,1)S(1)} %bitcast.40), channel_id=1, source_target_pairs={{0,16},{4,20},{8,24},{12,28},{16,0},{20,4},{24,8},{28,12},{1,17},{... | collective-permute-start | bytes 294920 | tf_op jit(solution)/shard_map/ppermute | solution.py:406
  31.3 5.6 %collective-permute-start.6 = (bf16[2,8,768]{2,1,0:T(8,128)(2,1)S(1)}, bf16[2,8,768]{2,1,0:T(8,128)(2,1)S(1)}, u32[]{:S(2)}, u32[]{:S(2)}) collective-permute-start(bf16[2,8,768]{2,1,0:T(8,128)(2,1)S(1)} %get-tuple-element.89), channel_id=1, source_target_pairs={{0,8},{4,12},{8,0},{12,4},{16,24},{20,28},{24,16},{28,20},{1,9},{5... | collective-permute-start | bytes 73736 | tf_op jit(solution)/shard_map/ppermute | solution.py:406
  33.9 6.9 %collective-permute-start.2 = (bf16[144,768]{1,0:T(8,128)(2,1)S(1)}, bf16[144,768]{1,0:T(8,128)(2,1)S(1)}, u32[]{:S(2)}, u32[]{:S(2)}) collective-permute-start(bf16[144,768]{1,0:T(8,128)(2,1)S(1)} %pad_maximum_fusion.2), channel_id=1, source_target_pairs={{0,3},{1,0},{2,1},{3,2},{4,7},{5,4},{6,5},{7,6},{8,11},{9,8},{10,9... | collective-permute-start | bytes 663560 | tf_op jit(solution)/shard_map/ppermute | solution.py:388
  36.7 7.2 %collective-permute-start.1 = (bf16[144,768]{1,0:T(8,128)(2,1)S(1)}, bf16[144,768]{1,0:T(8,128)(2,1)S(1)}, u32[]{:S(2)}, u32[]{:S(2)}) collective-permute-start(bf16[144,768]{1,0:T(8,128)(2,1)S(1)} %pad_maximum_fusion.1), channel_id=1, source_target_pairs={{0,1},{1,2},{2,3},{3,0},{4,5},{5,6},{6,7},{7,4},{8,9},{9,10},{10,1... | collective-permute-start | bytes 663560 | tf_op jit(solution)/shard_map/ppermute | solution.py:388
  36.9 3.9 %collective-permute-start.7 = (bf16[1,16,768]{2,1,0:T(8,128)(2,1)S(1)}, bf16[1,16,768]{2,1,0:T(8,128)(2,1)S(1)}, u32[]{:S(2)}, u32[]{:S(2)}) collective-permute-start(bf16[1,16,768]{2,1,0:T(8,128)(2,1)S(1)} %get-tuple-element.87), channel_id=1, source_target_pairs={{0,4},{4,0},{8,12},{12,8},{16,20},{20,16},{24,28},{28,24},{1,5},{5... | collective-permute-start | bytes 73736 | tf_op jit(solution)/shard_map/ppermute | solution.py:406
  45.0 20.9 %collective-permute-start.9 = (bf16[864,768]{1,0:T(8,128)(2,1)S(1)}, bf16[864,768]{1,0:T(8,128)(2,1)}, u32[]{:S(2)}, u32[]{:S(2)}) collective-permute-start(bf16[864,768]{1,0:T(8,128)(2,1)S(1)} %pad_maximum_fusion.here_ref), channel_id=1, source_target_pairs={{0,240},{4,244},{8,248},{12,252},{16,224},{20,228},{24,232},{28,23... | collective-permute-start | bytes 3981320 | tf_op jit(solution)/shard_map/ppermute | solution.py:401
  45.0 20.9 %collective-permute-start.8 = (bf16[864,768]{1,0:T(8,128)(2,1)S(1)}, bf16[864,768]{1,0:T(8,128)(2,1)}, u32[]{:S(2)}, u32[]{:S(2)}) collective-permute-start(bf16[864,768]{1,0:T(8,128)(2,1)S(1)} %pad_maximum_fusion.here_ref), channel_id=1, source_target_pairs={{0,32},{4,36},{8,40},{12,44},{16,48},{20,52},{24,56},{28,60},{32,6... | collective-permute-start | bytes 3981320 | tf_op jit(solution)/shard_map/ppermute | solution.py:401
  47.0 15.9 %all-to-all-start.1 = ((bf16[4,128,768]{2,1,0:T(8,128)(2,1)}), bf16[4,128,768]{2,1,0:T(8,128)(2,1)S(1)}, u32[]{:S(2)}, u32[]{:S(2)}) async-start(bf16[4,128,768]{2,1,0:T(8,128)(2,1)} %shard_map.164), calls=%async_computation.1 | async-start | bytes 1572864 | tf_op jit(solution)/shard_map/all_to_all | solution.py:412
  50.5 5.7 %collective-permute-start.10 = (bf16[1,32,768]{2,1,0:T(8,128)(2,1)S(1)}, bf16[1,32,768]{2,1,0:T(8,128)(2,1)S(1)}, u32[]{:S(2)}, u32[]{:S(2)}) collective-permute-start(bf16[1,32,768]{2,1,0:T(8,128)(2,1)S(1)} %pad_maximum_fusion.9), channel_id=1, source_target_pairs={{0,2},{1,3},{2,0},{3,1},{4,6},{5,7},{6,4},{7,5},{8,10},{9,11},{10,... | collective-permute-start | bytes 147464 | tf_op jit(solution)/shard_map/ppermute | solution.py:406
  56.2 5.7 %collective-permute-start.11 = (bf16[1,64,768]{2,1,0:T(8,128)(2,1)S(1)}, bf16[1,64,768]{2,1,0:T(8,128)(2,1)S(1)}, u32[]{:S(2)}, u32[]{:S(2)}) collective-permute-start(bf16[1,64,768]{2,1,0:T(8,128)(2,1)S(1)} %pad_maximum_fusion.4), channel_id=1, source_target_pairs={{0,1},{1,0},{2,3},{3,2},{4,5},{5,4},{6,7},{7,6},{8,9},{9,8},{10,11... | collective-permute-start | bytes 294920 | tf_op jit(solution)/shard_map/ppermute | solution.py:406
  63.0 2.1 %collective-permute-start.12 = (bf16[1,128,768]{2,1,0:T(8,128)(2,1)S(1)}, bf16[1,128,768]{2,1,0:T(8,128)(2,1)S(1)}, u32[]{:S(2)}, u32[]{:S(2)}) collective-permute-start(bf16[1,128,768]{2,1,0:T(8,128)(2,1)S(1)} %pad_maximum_fusion.3), channel_id=1, source_target_pairs={{0,32},{32,0},{64,96},{96,64},{128,160},{160,128},{192,224},{224,1... | collective-permute-start | bytes 589832 | tf_op jit(solution)/shard_map/ppermute | solution.py:406
  79.8 6.1 %collective-permute-start.20 = (f32[1,128,768]{2,1,0:T(8,128)}, f32[1,128,768]{2,1,0:T(8,128)S(1)}, u32[]{:S(2)}, u32[]{:S(2)}) collective-permute-start(f32[1,128,768]{2,1,0:T(8,128)} %bitcast.46), channel_id=1, source_target_pairs={{0,32},{32,0},{64,96},{96,64},{128,160},{160,128},{192,224},{224,1... | collective-permute-start | bytes 1179656 | tf_op jit(solution)/shard_map/ppermute | solution.py:406
  80.5 9.1 %collective-permute-start.13 = (bf16[352,768]{1,0:T(8,128)(2,1)}, bf16[352,768]{1,0:T(8,128)(2,1)S(1)}, u32[]{:S(2)}, u32[]{:S(2)}) collective-permute-start(bf16[352,768]{1,0:T(8,128)(2,1)} %get-tuple-element.47), channel_id=1, source_target_pairs={{0,240},{4,244},{8,248},{12,252},{16,224},{20,228},{24,232},{28,23... | collective-permute-start | bytes 1622024 | tf_op jit(solution)/shard_map/ppermute | solution.py:401
  82.4 9.0 %collective-permute-start.14 = (bf16[352,768]{1,0:T(8,128)(2,1)}, bf16[352,768]{1,0:T(8,128)(2,1)S(1)}, u32[]{:S(2)}, u32[]{:S(2)}) collective-permute-start(bf16[352,768]{1,0:T(8,128)(2,1)} %get-tuple-element.48), channel_id=1, source_target_pairs={{0,32},{4,36},{8,40},{12,44},{16,48},{20,52},{24,56},{28,60},{32,6... | collective-permute-start | bytes 1622024 | tf_op jit(solution)/shard_map/ppermute | solution.py:401
  82.4 17.1 %all-to-all-start.2 = ((bf16[4,128,768]{2,1,0:T(8,128)(2,1)}), bf16[4,128,768]{2,1,0:T(8,128)(2,1)S(1)}, u32[]{:S(2)}, u32[]{:S(2)}) async-start(bf16[4,128,768]{2,1,0:T(8,128)(2,1)} %get-tuple-element.42), calls=%async_computation.2 | async-start | bytes 1572864 | tf_op jit(solution)/shard_map/all_to_all | solution.py:412
  86.0 7.6 %collective-permute-start.21 = (f32[1,64,768]{2,1,0:T(8,128)S(1)}, f32[1,64,768]{2,1,0:T(8,128)S(1)}, u32[]{:S(2)}, u32[]{:S(2)}) collective-permute-start(f32[1,64,768]{2,1,0:T(8,128)S(1)} %slice.173), channel_id=1, source_target_pairs={{0,1},{1,0},{2,3},{3,2},{4,5},{5,4},{6,7},{7,6},{8,9},{9,8},{10,11... | collective-permute-start | bytes 589832 | tf_op jit(solution)/shard_map/ppermute | solution.py:406
  94.3 6.4 %collective-permute-start.22 = (f32[1,32,768]{2,1,0:T(8,128)}, f32[1,32,768]{2,1,0:T(8,128)}, u32[]{:S(2)}, u32[]{:S(2)}) collective-permute-start(f32[1,32,768]{2,1,0:T(8,128)} %get-tuple-element.72), channel_id=1, source_target_pairs={{0,2},{1,3},{2,0},{3,1},{4,6},{5,7},{6,4},{7,5},{8,10},{9,11},{10,... | collective-permute-start | bytes 294920 | tf_op jit(solution)/shard_map/ppermute | solution.py:406
  95.7 23.4 %collective-permute-start.15 = (bf16[512,768]{1,0:T(8,128)(2,1)}, bf16[512,768]{1,0:T(8,128)(2,1)S(1)}, u32[]{:S(2)}, u32[]{:S(2)}) collective-permute-start(bf16[512,768]{1,0:T(8,128)(2,1)} %get-tuple-element.49), channel_id=1, source_target_pairs={{0,240},{4,244},{8,248},{12,252},{16,224},{20,228},{24,232},{28,23... | collective-permute-start | bytes 2359304 | tf_op jit(solution)/shard_map/ppermute | solution.py:401
  95.7 23.4 %collective-permute-start.16 = (bf16[512,768]{1,0:T(8,128)(2,1)}, bf16[512,768]{1,0:T(8,128)(2,1)S(1)}, u32[]{:S(2)}, u32[]{:S(2)}) collective-permute-start(bf16[512,768]{1,0:T(8,128)(2,1)} %get-tuple-element.51), channel_id=1, source_target_pairs={{0,32},{4,36},{8,40},{12,44},{16,48},{20,52},{24,56},{28,60},{32,6... | collective-permute-start | bytes 2359304 | tf_op jit(solution)/shard_map/ppermute | solution.py:401
  96.2 9.7 %collective-permute-start.17 = (bf16[144,768]{1,0:T(8,128)(2,1)}, bf16[144,768]{1,0:T(8,128)(2,1)}, u32[]{:S(2)}, u32[]{:S(2)}) collective-permute-start(bf16[144,768]{1,0:T(8,128)(2,1)} %get-tuple-element.70), channel_id=1, source_target_pairs={{0,1},{1,2},{2,3},{3,0},{4,5},{5,6},{6,7},{7,4},{8,9},{9,10},{10,1... | collective-permute-start | bytes 663560 | tf_op jit(solution)/shard_map/ppermute | solution.py:388
  97.1 9.1 %collective-permute-start.18 = (bf16[144,768]{1,0:T(8,128)(2,1)}, bf16[144,768]{1,0:T(8,128)(2,1)}, u32[]{:S(2)}, u32[]{:S(2)}) collective-permute-start(bf16[144,768]{1,0:T(8,128)(2,1)} %get-tuple-element.71), channel_id=1, source_target_pairs={{0,3},{1,0},{2,1},{3,2},{4,7},{5,4},{6,5},{7,6},{8,11},{9,8},{10,9... | collective-permute-start | bytes 663560 | tf_op jit(solution)/shard_map/ppermute | solution.py:388
  101.7 11.8 %collective-permute-start.23 = (f32[1,16,768]{2,1,0:T(8,128)S(1)}, f32[1,16,768]{2,1,0:T(8,128)S(1)}, u32[]{:S(2)}, u32[]{:S(2)}) collective-permute-start(f32[1,16,768]{2,1,0:T(8,128)S(1)} %get-tuple-element.82), channel_id=1, source_target_pairs={{0,4},{4,0},{8,12},{12,8},{16,20},{20,16},{24,28},{28,24},{1,5},{5... | collective-permute-start | bytes 147464 | tf_op jit(solution)/shard_map/ppermute | solution.py:406
  107.7 11.4 %collective-permute-start.19 = (bf16[64,768]{1,0:T(8,128)(2,1)S(1)}, bf16[64,768]{1,0:T(8,128)(2,1)S(1)}, u32[]{:S(2)}, u32[]{:S(2)}) collective-permute-start(bf16[64,768]{1,0:T(8,128)(2,1)S(1)} %pad_maximum_fusion.5), channel_id=1, source_target_pairs={{0,16},{4,20},{8,24},{12,28},{16,0},{20,4},{24,8},{28,12},{1,17},{... | collective-permute-start | bytes 294920 | tf_op jit(solution)/shard_map/ppermute | solution.py:406
  113.4 5.7 %collective-permute-start.24 = (f32[2,8,768]{2,1,0:T(8,128)S(1)}, f32[2,8,768]{2,1,0:T(8,128)S(1)}, u32[]{:S(2)}, u32[]{:S(2)}) collective-permute-start(f32[2,8,768]{2,1,0:T(8,128)S(1)} %get-tuple-element.78), channel_id=1, source_target_pairs={{0,8},{4,12},{8,0},{12,4},{16,24},{20,28},{24,16},{28,20},{1,9},{5... | collective-permute-start | bytes 147464 | tf_op jit(solution)/shard_map/ppermute | solution.py:406
  119.2 4.2 %collective-permute-start.25 = (f32[4,4,768]{2,1,0:T(4,128)S(1)}, f32[4,4,768]{2,1,0:T(4,128)S(1)}, u32[]{:S(2)}, u32[]{:S(2)}) collective-permute-start(f32[4,4,768]{2,1,0:T(4,128)S(1)} %get-tuple-element.74), channel_id=1, source_target_pairs={{0,64},{32,96},{64,0},{96,32},{128,192},{160,224},{192,128},{224,1... | collective-permute-start | bytes 147464 | tf_op jit(solution)/shard_map/ppermute | solution.py:406
  123.4 5.8 %collective-permute-start.26 = (f32[4,2,768]{2,1,0:T(2,128)S(1)}, f32[4,2,768]{2,1,0:T(2,128)S(1)}, u32[]{:S(2)}, u32[]{:S(2)}) collective-permute-start(f32[4,2,768]{2,1,0:T(2,128)S(1)} %slice.183), channel_id=1, source_target_pairs={{0,128},{32,160},{64,192},{96,224},{128,0},{160,32},{192,64},{224,... | collective-permute-start | bytes 73736 | tf_op jit(solution)/shard_map/ppermute | solution.py:406
  124.8 15.7 %all-to-all-start.3 = ((bf16[4,128,768]{2,1,0:T(8,128)(2,1)}), bf16[4,128,768]{2,1,0:T(8,128)(2,1)S(1)}, u32[]{:S(2)}, u32[]{:S(2)}) async-start(bf16[4,128,768]{2,1,0:T(8,128)(2,1)} %shard_map.167), calls=%async_computation.3 | async-start | bytes 1572864 | tf_op jit(solution)/shard_map/all_to_all | solution.py:412
  129.3 7.7 %collective-permute-start.27 = (f32[4,1,768]{2,1,0:T(1,128)S(1)}, f32[4,1,768]{2,1,0:T(1,128)S(1)}, u32[]{:S(2)}, u32[]{:S(2)}) collective-permute-start(f32[4,1,768]{2,1,0:T(1,128)S(1)} %slice.185), channel_id=1, source_target_pairs={{0,16},{4,20},{8,24},{12,28},{16,0},{20,4},{24,8},{28,12},{1,17},{... | collective-permute-start | bytes 36872 | tf_op jit(solution)/shard_map/ppermute | solution.py:406
  (15 other events, 115.2 us)
